TPU v7x, 32 devices: a whole 2x2x4 slice. The times are simulated.
32 devices in a mesh: req: 16 (over z, y, x), tp: 2 (over core).
Axes of the slice: x: 2, y: 2, z: 4, core: 2. Of those that a mesh axis runs over, the one named last changes fastest.
Arguments:
- suffix_tokens: bfloat16 [256, 112, 2880], P('req'), may hold values from -40 to 40
- route_lengths: int32 [16, 16], replicated, may hold values from 1 to 112, 768 in all within a row
- dest_perm: int32 [16, 16], replicated, may hold values from 0 to 15, each once within a row
- attach_points: int32 [256], replicated, may hold values from 256 to 8192
- prefix_cache: bfloat16 [64, 128, 8, 128], P('req', None, 'tp'), may hold values from -120 to 120
- block_of_slot: int32 [64], replicated, may hold values from 0 to 63, each once
- sink_logits: float32 [64], P('tp'), may hold values from 0 to 6
- attn_gain: bfloat16 [2880], replicated, may hold values from 0.099609375 to 1.8984375
- w_query: bfloat16 [2880, 4096], P(None, 'tp'), may hold values from -0.109375 to 0.109375
- w_keyval: bfloat16 [2880, 8, 128], P(None, 'tp'), may hold values from -0.109375 to 0.109375
- w_out: bfloat16 [4096, 2880], P('tp'), may hold values from -0.09375 to 0.09375
- mlp_gain: bfloat16 [2880], replicated, may hold values from 0.099609375 to 1.8984375
- w_gate: bfloat16 [2880, 2880], P(None, 'tp'), may hold values from -0.109375 to 0.109375
- w_up: bfloat16 [2880, 2880], P(None, 'tp'), may hold values from -0.109375 to 0.109375
- w_down: bfloat16 [2880, 2880], P('tp'), may hold values from -0.109375 to 0.109375
Outputs:
- layer_out: bfloat16 [256, 112, 2880], P('req', None, 'tp')
Inputs may be any that keep to these rules, and one draw needn't show every extreme that they name: `route_lengths`: each row sums to 768, and the largest entry of each row is 112. `dest_perm`: each row is a permutation of the devices of req. `block_of_slot`: a permutation.
All inputs are finite; a program needn't handle non-finite values.
Results may differ from a plain program's by a relative error of at most 0.013.
Values may be sent and summed in bfloat16 or wider, within the bound.
A program may use at most 256 MiB of HBM per device.

v0:
```python
import jax
import jax.numpy as jnp
from jax import lax
from jax.sharding import PartitionSpec as P

WINDOW = 128
CAP = 768


ROPE_BASE = 150000.0
EPSILON = 1e-05


def norm_rows(inputs, gains):
    widened = inputs.astype(jnp.float32)
    factor = lax.rsqrt(jnp.mean(widened * widened, axis=-1, keepdims=True) + EPSILON)
    return (widened * factor * gains.astype(jnp.float32)).astype(jnp.bfloat16)


def rotate(vectors, positions):
    half_dim = vectors.shape[-1] // 2
    frequency = ROPE_BASE ** (-(jnp.arange(half_dim).astype(jnp.float32) * 2.0 / vectors.shape[-1]))
    angles = positions.astype(jnp.float32)[:, None, None] * frequency
    cosine = jnp.cos(angles)
    sine_part = jnp.sin(angles)
    first_half = vectors[..., :half_dim]
    second = vectors[..., half_dim:]
    return jnp.concatenate(
        [first_half * cosine - second * sine_part, second * cosine + first_half * sine_part],
        axis=-1,
    )


def attend(query_slots, paired_slots, tail_rows, sink_logits):
    peers, slot_length = (query_slots.shape[0], query_slots.shape[1])
    value_heads = paired_slots.shape[2]
    head_dim = paired_slots.shape[3] // 2
    group_size = query_slots.shape[2] // value_heads
    window = tail_rows.shape[1]
    grouped_query = query_slots.reshape(peers, slot_length, value_heads, group_size, head_dim)
    near_keys = jnp.concatenate([tail_rows, paired_slots], axis=1)
    score_scale = head_dim ** (-0.5)
    near_scores = (
        jnp.einsum(
            "ntkgd,nskd->nkgts",
            grouped_query,
            near_keys[..., :head_dim],
            preferred_element_type=jnp.float32,
        )
        * score_scale
    )
    sink_scores = sink_logits.reshape(value_heads, group_size)[None, :, :, None, None]
    slot_steps = jnp.arange(slot_length)
    columns = jnp.arange(window + slot_length)
    allowed = jnp.where(
        columns[None, :] < window,
        columns[None, :] > slot_steps[:, None],
        columns[None, :] - window <= slot_steps[:, None],
    )
    near_scores = jnp.where(allowed, near_scores, -jnp.inf)
    largest = jnp.maximum(jnp.max(near_scores, axis=-1, keepdims=True), sink_scores)
    near_weights = jnp.exp(near_scores - largest)
    normalizer = jnp.sum(near_weights, axis=-1, keepdims=True) + jnp.exp(sink_scores - largest)
    near_weights = (near_weights / normalizer).astype(jnp.bfloat16)
    mixed = jnp.einsum(
        "nkgts,nskd->ntkgd",
        near_weights,
        near_keys[..., head_dim:],
        preferred_element_type=jnp.float32,
    )
    return mixed.astype(jnp.bfloat16).reshape(
        peers * slot_length, value_heads * group_size * head_dim
    )


def fetch_prefix(attach_slots, prefix_cache, block_of_slot, window):
    total_blocks = block_of_slot.shape[0]
    block_len = prefix_cache.shape[1]
    catalog = jnp.arange(total_blocks)
    home_row = jnp.sum(
        jnp.where(block_of_slot[None, :] == catalog[:, None], catalog[None, :], 0), axis=1
    )
    wanted = attach_slots[:, None] - window + jnp.arange(window)[None, :]
    block_id = wanted // block_len
    tail_store = jnp.sum(jnp.where(block_id[..., None] == catalog, home_row, 0), axis=-1)
    tail_offset = wanted - block_id * block_len
    trailing = prefix_cache.shape[2:]
    initial = jnp.zeros((attach_slots.shape[0], window) + trailing, jnp.bfloat16)
    shard_rows = lax.all_gather(prefix_cache, "req", axis=0, tiled=True)
    held_blocks = shard_rows.shape[0]
    flat_rows = shard_rows.reshape((held_blocks * block_len,) + trailing)
    inside = (tail_store >= 0) & (tail_store < held_blocks)
    picked = flat_rows[jnp.clip(tail_store, 0, held_blocks - 1) * block_len + tail_offset]
    return jnp.where(inside[..., None, None], picked, initial)


def local(
    suffix_tokens,
    route_lengths,
    dest_perm,
    attach_points,
    prefix_cache,
    block_of_slot,
    sink_logits,
    attn_gain,
    w_query,
    w_keyval,
    w_out,
    mlp_gain,
    w_gate,
    w_up,
    w_down,
):
    peers = lax.axis_size("req")
    splits = lax.axis_size("tp")
    request_index = lax.axis_index("req")
    tensor_index = lax.axis_index("tp")
    slot_count, slot_length, features = suffix_tokens.shape
    feature_share = features // splits
    value_heads = w_keyval.shape[1]
    head_dim = w_keyval.shape[2] // 2
    peer_ids = jnp.arange(peers)
    slot_steps = jnp.arange(slot_length)
    my_row = lax.dynamic_index_in_dim(dest_perm, request_index, 0, keepdims=False)
    attach_table = attach_points.reshape(peers, peers)
    arriving_lengths = lax.dynamic_index_in_dim(route_lengths, request_index, 0, keepdims=False)
    arriving = (dest_perm == request_index).astype(jnp.int32)
    arriving_attach = jnp.sum(attach_table * arriving, axis=1)
    send_order = jnp.sum(
        jnp.where(my_row[None, :] == peer_ids[:, None], peer_ids[None, :], 0), axis=1
    )
    run_ends = jnp.cumsum(arriving_lengths)
    starts = run_ends - arriving_lengths
    packed_ids = jnp.arange(CAP)
    source_of = jnp.sum((run_ends[None, :] <= packed_ids[:, None]).astype(jnp.int32), axis=1)
    source_hot = (source_of[:, None] == peer_ids[None, :]).astype(jnp.int32)
    token_index = packed_ids - jnp.sum(source_hot * starts[None, :], axis=1)
    positions = jnp.sum(source_hot * arriving_attach[None, :], axis=1) + token_index
    flat_index = source_of * slot_length + token_index
    slot_source = jnp.clip(starts[:, None] + slot_steps[None, :], 0, CAP - 1).reshape(-1)
    live_mask = slot_steps[None, :] < arriving_lengths[:, None]

    def to_slots(values):
        return values[slot_source].reshape((peers, slot_length) + values.shape[1:])

    tail_rows = fetch_prefix(arriving_attach, prefix_cache, block_of_slot, WINDOW)
    landed = lax.all_to_all(
        suffix_tokens[send_order], "req", split_axis=0, concat_axis=0, tiled=True
    )
    input_rows = landed.reshape(peers * slot_length, features)[flat_index]
    row_total = input_rows.shape[0]
    normed_in = norm_rows(input_rows, attn_gain)
    queries = jnp.dot(normed_in, w_query, preferred_element_type=jnp.float32).reshape(
        row_total, -1, head_dim
    )
    queries = rotate(queries, positions).astype(jnp.bfloat16)
    paired = jnp.dot(
        normed_in, w_keyval.reshape(features, -1), preferred_element_type=jnp.float32
    ).reshape(row_total, value_heads, 2 * head_dim)
    rotated = rotate(paired[..., :head_dim], positions)
    paired = jnp.concatenate([rotated, paired[..., head_dim:]], axis=-1).astype(jnp.bfloat16)
    attended = attend(to_slots(queries), to_slots(paired), tail_rows, sink_logits)[flat_index]
    partial_value = jnp.dot(attended, w_out, preferred_element_type=jnp.float32)
    summed = lax.psum(partial_value.astype(jnp.bfloat16), "tp").astype(jnp.float32)
    residual = (input_rows.astype(jnp.float32) + summed).astype(jnp.bfloat16)
    normed_mid = norm_rows(residual, mlp_gain)
    residual_part = lax.dynamic_slice_in_dim(
        residual, tensor_index * feature_share, feature_share, 1
    )
    gate_proj = jnp.dot(normed_mid, w_gate, preferred_element_type=jnp.float32)
    up_proj = jnp.dot(normed_mid, w_up, preferred_element_type=jnp.float32)
    hidden = (jax.nn.silu(gate_proj) * up_proj).astype(jnp.bfloat16)
    down_sum = lax.psum_scatter(
        jnp.dot(hidden, w_down, preferred_element_type=jnp.float32).astype(jnp.bfloat16),
        "tp",
        scatter_dimension=1,
        tiled=True,
    ).astype(jnp.float32)
    out_rows = (residual_part.astype(jnp.float32) + down_sum).astype(jnp.bfloat16)
    out_slots = jnp.where(live_mask[..., None], to_slots(out_rows), jnp.zeros((), jnp.bfloat16))
    returned = lax.all_to_all(out_slots, "req", split_axis=0, concat_axis=0, tiled=True)
    return returned[my_row]


def solution(mesh):
    in_specs = (
        P("req", None, None),
        P(),
        P(),
        P(),
        P("req", None, "tp", None),
        P(),
        P("tp"),
        P(),
        P(None, "tp"),
        P(None, "tp", None),
        P("tp", None),
        P(),
        P(None, "tp"),
        P(None, "tp"),
        P("tp", None),
    )
    out_specs = P("req", None, "tp")
    return jax.shard_map(local, mesh=mesh, in_specs=in_specs, out_specs=out_specs, check_vma=False)
```

profile of v0, /device:TPU:14, one launch (start us, length us, event | category | flops | bytes accessed | tf_op | source)
XLA Modules:
  0.0 870.4 jit_solution(7869637061355180574)
XLA Ops:
  7.4 9.7 %gather_fusion = bf16[16,112,2880]{2,1,0:T(8,128)(2,1)} fusion(bf16[16,112,2880]{2,1,0:T(8,128)(2,1)} %param.15, s32[1024]{0:T(1024)S(1)} %pad_clamp_fusion.3), kind=kCustom, calls=%fused_computation | custom fusion | bytes 20643904 | tf_op jit(solution)/shard_map/gather | solution.py:148
  17.0 7.4 all-to-all-start
  24.5 0.9 copy.77
  25.5 0.7 fusion.61
  26.5 4.5 copy.104
  32.2 0.7 fusion.45
  33.6 0.9 copy.90
  35.3 281.4 %all-gather.2.cloned.1.call-done = bf16[64,128,4,128]{3,1,2,0:T(8,128)(2,1)} async-done(((bf16[4,128,4,128]{3,1,2,0:T(8,128)(2,1)}), bf16[64,128,4,128]{3,1,2,0:T(8,128)(2,1)}) %all-gather.2.cloned.1.call-update) | async-done | bytes 8388624 | tf_op jit(solution)/shard_map/all_gather | solution.py:89
  316.7 11.1 %copy.78 = bf16[64,128,4,128]{3,2,1,0:T(4,128)(2,1)} copy(bf16[64,128,4,128]{3,1,2,0:T(8,128)(2,1)} %all-gather.2.cloned.1.call-done) | data formatting | bytes 16777216 | tf_op jit(solution)/shard_map/all_gather | solution.py:89
  327.7 10.2 %gather_fusion.2 = bf16[2048,4,128]{2,1,0:T(4,128)(2,1)S(1)} fusion(bf16[8192,4,128]{2,1,0:T(4,128)(2,1)} %bitcast.89, s32[2048]{0:T(1024)S(1)} %fusion.36), kind=kCustom, calls=%fused_computation.2 | custom fusion | bytes 4202496 | tf_op jit(solution)/shard_map/gather | solution.py:93
  338.0 2.4 copy.80
  340.3 1.7 broadcast_select_fusion.1
  342.1 14.6 %gather_fusion.1 = bf16[768,2880]{1,0:T(8,128)(2,1)} fusion(bf16[1792,2880]{1,0:T(8,128)(2,1)} %bitcast.4, s32[1024]{0:T(1024)S(1)} %pad_clamp_fusion.2), kind=kCustom, calls=%fused_computation.1 | custom fusion | bytes 8850432 | tf_op jit(solution)/shard_map/gather | solution.py:150
  356.7 6.7 copy.76
  363.4 3.2 fusion.8
  366.6 6.0 fusion.12
  372.8 0.9 pad_maximum_fusion.2
  373.7 1.5 copy.83
  375.2 6.3 gather_fusion.3
  381.5 4.1 copy.85
  385.6 15.7 %fusion.22 = f32[768,2048]{0,1:T(8,128)S(1)} fusion(bf16[2880,2048]{1,0:T(8,128)(2,1)} %param.23, bf16[768,2880]{0,1:T(8,128)(2,1)} %copy.76, f32[2880]{0:T(1024)S(1)} %convert_element_type.77, f32[768]{0:T(1024)S(1)} %add_rsqrt_fusion.1), kind=kOutput, calls=%fused_computation.49 | convolution fusion | flops 9068544000 | bytes 22526208 | tf_op jit(solution)/shard_map/dot_general | solution.py:153
  401.2 3.1 fusion.53
  404.4 11.3 %copy.111 = f32[768,32,32]{2,1,0:T(8,128)} copy(f32[768,32,32]{0,2,1:T(8,128)} %get-tuple-element.12) | data formatting | bytes 6291456
  415.7 11.4 %copy.112 = f32[768,32,32]{2,1,0:T(8,128)} copy(f32[768,32,32]{0,2,1:T(8,128)} %get-tuple-element.11) | data formatting | bytes 6291456
  427.1 9.7 %subtract_convert_fusion = (bf16[768,32,32]{2,1,0:T(8,128)(2,1)S(1)}, bf16[768,32,32]{2,1,0:T(8,128)(2,1)S(1)}) fusion(f32[768,32,32]{2,1,0:T(8,128)} %copy.112, f32[768,32,32]{2,1,0:T(8,128)} %copy.111, f32[768,32]{1,0:T(8,128)S(1)} %copy-done.3, f32[768,32]{1,0:T(8,128)S(1)} %copy.88), kind=kLoop, calls=%fused_computation.20 | loop fusion | flops 6291456 | bytes 9633792 | tf_op jit(solution)/shard_map/convert
  436.8 5.0 pad_maximum_fusion
  441.8 11.1 %gather_fusion.4 = bf16[1792,32,64]{2,1,0:T(8,128)(2,1)} fusion(bf16[768,32,64]{2,1,0:T(8,128)(2,1)} %pad_maximum_fusion, s32[2048]{0:T(1024)S(1)} %pad_clamp_fusion), kind=kCustom, calls=%fused_computation.4 | custom fusion | bytes 14687232 | tf_op jit(solution)/shard_map/gather | solution.py:144
  452.9 3.2 fusion.65
  456.1 28.1 %fusion.1 = (f32[16,4,8,112]{3,2,1,0:T(8,128)S(1)}, f32[16,4,240,112,8]{2,3,4,1,0:T(8,128)}) fusion(pred[112,240]{1,0:T(8,128)(4,1)S(1)} %fusion.29, bf16[16,112,4,8,64]{4,3,2,1,0:T(8,128)(2,1)} %bitcast.87, bf16[16,112,4,128]{1,3,2,0:T(8,128)(2,1)} %copy.85, bf16[16,128,4,128]{1,3,2,0:T(8,128)(2,1)S(1)} %broadcast_select_fusion.1), kind=kOutput, calls=%fused_computation.12 | convolution fusion | flops 1806770176 | bytes 66578688 | tf_op jit(solution)/shard_map/ntkgd,nskd->nkgts/dot_general | solution.py:44
  484.3 22.7 %fusion = f32[16,4,8,112]{3,2,1,0:T(8,128)S(1)} fusion(f32[16,4,240,112,8]{2,3,4,1,0:T(8,128)} %get-tuple-element.18, f32[16,4,8,112]{3,2,1,0:T(8,128)S(1)} %broadcast_maximum_fusion, pred[112,240]{1,0:T(8,128)(4,1)S(1)} %fusion.29), kind=kLoop, calls=%fused_computation.11 | loop fusion | flops 54992896 | bytes 55535872 | tf_op jit(solution)/shard_map/reduce_sum | solution.py:63
  507.1 31.3 %convert_bitcast_fusion = bf16[16,112,4,8,64]{1,4,3,2,0:T(8,128)(2,1)} fusion(f32[16,4,240,112,8]{2,3,4,1,0:T(8,128)} %get-tuple-element.18, f32[16,4,8,112]{3,2,1,0:T(8,128)S(1)} %exponential_add_fusion, f32[16,4,8,112]{3,2,1,0:T(8,128)S(1)} %broadcast_maximum_fusion, pred[112,240]{1,0:T(8,128)(4,1)S(1)} %fusion.29, ...), kind=kOutput, calls=%fused_computation.30 | convolution fusion | flops 1834090496 | bytes 64841984 | tf_op jit(solution)/shard_map/nkgts,nskd->ntkgd/dot_general | solution.py:65
  538.4 22.4 %copy.109 = bf16[16,112,4,8,64]{4,3,2,1,0:T(8,128)(2,1)} copy(bf16[16,112,4,8,64]{1,4,3,2,0:T(8,128)(2,1)} %convert_bitcast_fusion) | data formatting | bytes 14680064 | tf_op jit(solution)/shard_map/reshape | solution.py:71
  560.8 20.8 %reshape.513 = bf16[1792,2048]{1,0:T(8,128)(2,1)} reshape(bf16[16,112,4,8,64]{4,3,2,1,0:T(8,128)(2,1)} %copy.109) | data formatting | bytes 14680064 | tf_op jit(solution)/shard_map/reshape | solution.py:71
  581.6 10.6 %gather_fusion.5 = bf16[768,2048]{1,0:T(8,128)(2,1)S(1)} fusion(bf16[1792,2048]{1,0:T(8,128)(2,1)} %reshape.513, s32[1024]{0:T(1024)S(1)} %copy-done.8), kind=kCustom, calls=%fused_computation.5 | custom fusion | bytes 6294528 | tf_op jit(solution)/shard_map/gather | solution.py:162
  592.2 13.7 %convolution_convert_fusion.1 = bf16[768,2880]{0,1:T(8,128)(2,1)} fusion(bf16[768,2048]{1,0:T(8,128)(2,1)S(1)} %gather_fusion.5, bf16[2048,2880]{0,1:T(8,128)(2,1)} %param.25), kind=kOutput, calls=%fused_computation.34 | convolution fusion | flops 9061908480 | bytes 19365888 | tf_op jit(solution)/shard_map/dot_general | solution.py:163
  606.0 31.4 %all-reduce.2.cloned.1.call-done = bf16[768,2880]{0,1:T(8,128)(2,1)} async-done(((bf16[768,2880]{0,1:T(8,128)(2,1)}), bf16[768,2880]{0,1:T(8,128)(2,1)}) %all-reduce.2.cloned.1.call-update) | async-done | bytes 4423696 | tf_op jit(solution)/shard_map/psum | solution.py:164
  637.4 5.4 fusion.5
  642.8 2.0 copy-done
  644.8 11.4 %fusion.25 = f32[768,1440]{0,1:T(8,128)} fusion(bf16[2880,1440]{0,1:T(8,128)(2,1)} %param.27, bf16[768,2880]{0,1:T(8,128)(2,1)S(1)} %get-tuple-element.8, f32[2880]{0:T(1024)S(1)} %convert_element_type.89, f32[768]{0:T(1024)S(1)} %add_rsqrt_fusion), kind=kOutput, calls=%fused_computation.50 | convolution fusion | flops 6378946560 | bytes 17156352 | tf_op jit(solution)/shard_map/dot_general | solution.py:170
  656.2 35.7 %convolution_convert_fusion = bf16[768,2880]{0,1:T(8,128)(2,1)} fusion(bf16[1440,2880]{1,0:T(8,128)(2,1)} %param.29, f32[768,1440]{0,1:T(8,128)} %fusion.25, bf16[2880,1440]{0,1:T(8,128)(2,1)} %param.28, bf16[768,2880]{0,1:T(8,128)(2,1)} %copy-done, f32[2880]{0:T(1024)S(1)} %convert_element_type.89, f32[768]{0:T(1024)S(1)} %add_rsqrt_fusion), kind=kOutput, calls=%fused_computation.33 | convolution fusion | flops 12757893120 | bytes 29874432 | tf_op jit(solution)/shard_map/dot_general | solution.py:174
  692.7 12.9 %reduce-scatter.2.cloned.1.call-done = bf16[768,1440]{0,1:T(8,128)(2,1)} async-done(((bf16[768,2880]{0,1:T(8,128)(2,1)}), bf16[768,1440]{0,1:T(8,128)(2,1)}) %reduce-scatter.2.cloned.1.call-update) | async-done | bytes 2211856 | tf_op jit(solution)/shard_map/reduce_scatter | solution.py:173
  705.6 4.2 add_convert_fusion.1
  709.8 2.8 copy.95
  712.6 7.1 gather_fusion.6
  719.7 5.5 broadcast_select_fusion
  725.1 7.0 all-to-all-start.1
  732.8 124.8 %all-to-all-done.1 = bf16[16,112,1440]{2,1,0:T(8,128)(2,1)} async-done(((bf16[16,112,1440]{2,1,0:T(8,128)(2,1)}), bf16[16,112,1440]{2,1,0:T(8,128)(2,1)}, u32[]{:S(2)}, u32[]{:S(2)}) %all-to-all-start.1) | async-done | bytes 5160992 | tf_op jit(solution)/shard_map/all_to_all | solution.py:181
  857.6 5.9 gather_fusion.7
  (81 shorter events, 5.6 us)
Async XLA Ops:
  17.0 7.5 copy-start.4
  17.0 9.4 %copy-start.12 = (s32[256]{0:T(256)S(1)}, s32[256]{0:T(256)}, u32[]{:S(2)}) copy-start(s32[256]{0:T(256)} %param.18) | copy-start | bytes 3076
  17.0 9.5 %copy-start.10 = (bf16[2880]{0:T(1024)(128)(2,1)S(1)}, bf16[2880]{0:T(1024)(128)(2,1)}, u32[]{:S(2)}) copy-start(bf16[2880]{0:T(1024)(128)(2,1)} %param.22) | copy-start | bytes 17284
  17.0 9.5 %copy-start.1 = (bf16[2880,4,128]{2,1,0:T(4,128)(2,1)S(1)}, bf16[2880,4,128]{2,1,0:T(4,128)(2,1)}, u32[]{:S(2)}) copy-start(bf16[2880,4,128]{2,1,0:T(4,128)(2,1)} %param.24) | copy-start | bytes 8847364
  17.0 325.0 %all-to-all-start = ((bf16[16,112,2880]{2,1,0:T(8,128)(2,1)}), bf16[16,112,2880]{2,1,0:T(8,128)(2,1)}, u32[]{:S(2)}, u32[]{:S(2)}) async-start(bf16[16,112,2880]{2,1,0:T(8,128)(2,1)} %gather_fusion), calls=%async_computation | async-start | bytes 21102592 | tf_op jit(solution)/shard_map/all_to_all | solution.py:147
  24.4 7.5 copy-start.9
  24.5 10.1 %copy-start.13 = (f32[32]{0:T(128)S(1)}, f32[32]{0:T(128)}, u32[]{:S(2)}) copy-start(f32[32]{0:T(128)} %param.21) | copy-start | bytes 388
  24.5 10.3 %copy-start.14 = (s32[64]{0:T(128)S(1)}, s32[64]{0:T(128)}, u32[]{:S(2)}) copy-start(s32[64]{0:T(128)} %param.20) | copy-start | bytes 772
  24.5 292.2 %all-gather.2.cloned.1.call-start = ((), (), s32[]{:S(2)}) async-start(), calls=%async_computation.3 | async-start | bytes 8912896 | tf_op jit(solution)/shard_map/all_gather | solution.py:89
  25.5 611.9 %all-reduce.2.cloned.1.call-start = ((), (), s32[]{:S(2)}) async-start(), calls=%async_computation.4 | async-start | bytes 8847360 | tf_op jit(solution)/shard_map/psum | solution.py:164
  34.7 307.4 %copy-start.7 = (s32[1024]{0:T(1024)}, s32[1024]{0:T(1024)S(1)}, u32[]{:S(2)}) copy-start(s32[1024]{0:T(1024)S(1)} %pad_clamp_fusion.2) | copy-start | bytes 12292
  34.7 407.1 %copy-start.5 = (s32[2048]{0:T(1024)}, s32[2048]{0:T(1024)S(1)}, u32[]{:S(2)}) copy-start(s32[2048]{0:T(1024)S(1)} %pad_clamp_fusion) | copy-start | bytes 24580
  415.7 11.4 %copy-start.3 = (f32[768,32]{1,0:T(8,128)S(1)}, f32[768,32]{1,0:T(8,128)}, u32[]{:S(2)}) copy-start(f32[768,32]{1,0:T(8,128)} %copy.90) | copy-start | bytes 294916
  484.2 22.9 %copy-start.2 = (bf16[16,240,4,64,1]{1,3,4,2,0:T(8,128)(2,1)S(1)}, bf16[16,240,4,64,1]{1,3,4,2,0:T(8,128)(2,1)}, u32[]{:S(2)}) copy-start(bf16[16,240,4,64,1]{1,3,4,2,0:T(8,128)(2,1)} %fusion.65) | copy-start | bytes 5898244
  560.8 20.8 %copy-start.8 = (s32[1024]{0:T(1024)S(1)}, s32[1024]{0:T(1024)}, u32[]{:S(2)}) copy-start(s32[1024]{0:T(1024)} %copy-done.7) | copy-start | bytes 12292
  592.2 13.7 %copy-start.11 = (bf16[2880]{0:T(1024)(128)(2,1)S(1)}, bf16[2880]{0:T(1024)(128)(2,1)}, u32[]{:S(2)}) copy-start(bf16[2880]{0:T(1024)(128)(2,1)} %param.26) | copy-start | bytes 17284
  605.9 99.7 %reduce-scatter.2.cloned.1.call-start = ((), (), s32[]{:S(2)}) async-start(), calls=%async_computation.5 | async-start | bytes 6635520 | tf_op jit(solution)/shard_map/reduce_scatter | solution.py:173
  642.7 2.0 copy-start
  692.7 19.9 %copy-start.6 = (s32[2048]{0:T(1024)S(1)}, s32[2048]{0:T(1024)}, u32[]{:S(2)}) copy-start(s32[2048]{0:T(1024)} %copy-done.5) | copy-start | bytes 24580
  725.1 132.4 %all-to-all-start.1 = ((bf16[16,112,1440]{2,1,0:T(8,128)(2,1)}), bf16[16,112,1440]{2,1,0:T(8,128)(2,1)}, u32[]{:S(2)}, u32[]{:S(2)}) async-start(bf16[16,112,1440]{2,1,0:T(8,128)(2,1)} %broadcast_select_fusion), calls=%async_computation.2 | async-start | bytes 11010048 | tf_op jit(solution)/shard_map/all_to_all | solution.py:181
Sparse Core Ops, SparseCore 0:
  28.1 288.5 all-gather.1
  606.0 31.3 all-reduce.1
  692.1 13.4 reduce-scatter.1
where the time goes:
time: 882 us; the launch traced here: 870 us
  waiting for transfers between devices  451 us (51%)
  local copies, waits for them, and re-layouts  184 us (21%)
  matrix products  142 us (16%)
  other arithmetic  65.6 us (7%)
  starting transfers between devices  14.5 us (2%)
  between operations  13.9 us (2%)
    all_gather x1, waiting for transfers between devices, fetch_prefix(): shard_rows = lax.all_gather(prefix_cache, 'req', axis=0, tiled=True)  281 us
    all_to_all x1, waiting for transfers between devices, local(): lax.all_to_all(out_slots, 'req', split_axis=0, concat_axis=0, tiled=True)  125 us
    reshape x2, local copies, waits for them, and re-layouts, attend(): mixed.astype(jnp.bfloat16)  43.2 us
    dot_general x1, matrix products, local(): jnp.dot(hidden, w_down, preferred_element_type=jnp.float32)  35.7 us
    psum x1, waiting for transfers between devices, local(): lax.psum(partial_value.astype(jnp.bfloat16), 'tp').astype(jnp.float32)  31.4 us
    dot_general x1, matrix products, attend(): jnp.einsum('nkgts,nskd->ntkgd', near_weights, near_keys[..., head_dim:],...  31.3 us
    dot_general x1, matrix products, attend(): jnp.einsum('ntkgd,nskd->nkgts', grouped_query, near_keys[..., :head_dim],...  28.1 us
    unnamed x33, local copies, waits for them, and re-layouts  25.7 us
  transfers between devices with their start and end apart: 5, of which 4 were waited for; matrix products, arithmetic and copies ran while one was open for 4% of the time, Pallas kernels for 0%

commit v1 on v0

v1 whole, which is shorter than its diff:
```python
import jax
import jax.numpy as jnp
from jax import lax
from jax.experimental import pallas as pl
from jax.experimental.pallas import tpu as pltpu
from jax.sharding import PartitionSpec as P

WINDOW = 128
CAP = 768


ROPE_BASE = 150000.0
EPSILON = 1e-05


def norm_rows(inputs, gains):
    widened = inputs.astype(jnp.float32)
    factor = lax.rsqrt(jnp.mean(widened * widened, axis=-1, keepdims=True) + EPSILON)
    return (widened * factor * gains.astype(jnp.float32)).astype(jnp.bfloat16)


CHUNK = 32
ALIGN = 8


def swap_halves(tile, lane):
    return jnp.where(lane % 64 < 32, pltpu.roll(tile, 96, 1), pltpu.roll(tile, 32, 1))


def attend_kernel(
    home_ref, offset_ref, start_ref, length_ref,
    query_ref, paired_ref, cosine_ref, sine_ref, sink_ref, prefix_ref,
    out_ref, blocks, tables, mixed, sems,
):
    peers = start_ref.shape[0]
    rows = query_ref.shape[0]
    heads = paired_ref.shape[1] // 128
    group_tiles = query_ref.shape[1] // 128 // heads

    def block_copy(n, half):
        return pltpu.make_async_copy(
            prefix_ref.at[home_ref[n, half]],
            blocks.at[n, pl.ds(half * WINDOW, WINDOW)],
            sems.at[n, half],
        )

    for n in range(peers):
        for half in range(2):
            block_copy(n, half).start()
    mixed[...] = jnp.zeros_like(mixed)

    lane = lax.broadcasted_iota(jnp.int32, (WINDOW, 128), 1)
    low = lane < 64

    def one_request(n, carry):
        start = pl.multiple_of(start_ref[n], ALIGN)
        length = length_ref[n]
        own = pl.multiple_of(jnp.minimum(start, rows - WINDOW), ALIGN)
        block_copy(n, 0).wait()
        block_copy(n, 1).wait()
        shift = (2 * WINDOW - offset_ref[n]) % (2 * WINDOW)
        cosine = cosine_ref[pl.ds(own, WINDOW), :]
        sine = sine_ref[pl.ds(own, WINDOW), :]
        for k in range(heads):
            columns = slice(k * 128, (k + 1) * 128)
            both = blocks[n, :, columns].astype(jnp.float32)
            fetched = pltpu.roll(both, shift, 0)[:WINDOW]
            fresh = paired_ref[pl.ds(own, WINDOW), columns]
            turned = fresh * cosine + swap_halves(fresh, lane) * sine
            fresh = jnp.where(low, turned, fresh)
            for part, tile in enumerate((fetched, fresh)):
                spot = slice(part * WINDOW, (part + 1) * WINDOW)
                moved = pltpu.roll(tile, 64, 1)
                tables[k, 0, spot] = jnp.where(low, tile, 0.0).astype(jnp.bfloat16)
                tables[k, 1, spot] = jnp.where(low, 0.0, moved).astype(jnp.bfloat16)
                tables[k, 2, spot] = jnp.where(low, moved, 0.0).astype(jnp.bfloat16)
                tables[k, 3, spot] = jnp.where(low, 0.0, tile).astype(jnp.bfloat16)

        shape = (group_tiles * CHUNK, 2 * WINDOW)
        step = lax.broadcasted_iota(jnp.int32, shape, 0) % CHUNK
        column = lax.broadcasted_iota(jnp.int32, shape, 1)
        own_step = column - WINDOW + (own - start)
        chunk_lane = lax.broadcasted_iota(jnp.int32, (CHUNK, 128), 1)

        def one_chunk(c, carry):
            first = pl.multiple_of(start + c * CHUNK, ALIGN)
            token = step + c * CHUNK
            allowed = ((column < WINDOW) & (column > token)) | (
                (column >= WINDOW) & (own_step >= 0) & (own_step <= token)
            )
            cosine = cosine_ref[pl.ds(first, CHUNK), :] * 0.125
            sine = sine_ref[pl.ds(first, CHUNK), :] * 0.125
            for k in range(heads):
                tiles = []
                for g in range(group_tiles):
                    at = (k * group_tiles + g) * 128
                    tile = query_ref[pl.ds(first, CHUNK), at : at + 128]
                    turned = tile * cosine + swap_halves(tile, chunk_lane) * sine
                    tiles.append(turned.astype(jnp.bfloat16))
                stacked = jnp.concatenate(tiles, axis=0)
                result = None
                for side in range(2):
                    score = lax.dot_general(
                        stacked, tables[k, side], (((1,), (1,)), ((), ())),
                        preferred_element_type=jnp.float32,
                    )
                    score = jnp.where(allowed, score, -jnp.inf)
                    sink = sink_ref[k, :, side : side + 1]
                    largest = jnp.maximum(jnp.max(score, axis=1, keepdims=True), sink)
                    weight = jnp.exp(score - largest)
                    total = jnp.sum(weight, axis=1, keepdims=True) + jnp.exp(sink - largest)
                    weight = (weight * (1.0 / total)).astype(jnp.bfloat16)
                    piece = jnp.dot(weight, tables[k, 2 + side], preferred_element_type=jnp.float32)
                    result = piece if result is None else result + piece
                for g in range(group_tiles):
                    at = (k * group_tiles + g) * 128
                    mixed[pl.ds(first, CHUNK), at : at + 128] = result[g * CHUNK : (g + 1) * CHUNK]
            return carry

        lax.fori_loop(0, (length + CHUNK - 1) // CHUNK, one_chunk, 0)
        return carry

    lax.fori_loop(0, peers, one_request, 0)

    def settle(i, carry):
        at = pl.multiple_of(i * 16, 16)
        out_ref[pl.ds(at, 16), :] = mixed[pl.ds(at, 16), :].astype(jnp.bfloat16)
        return carry

    lax.fori_loop(0, rows // 16, settle, 0)


def attend(queries, paired, cosine, sine, sinks, prefix, home, offsets, starts, lengths):
    peers = starts.shape[0]
    rows, width = queries.shape
    heads = paired.shape[1] // 128
    smem = pl.BlockSpec(memory_space=pltpu.SMEM)
    vmem = pl.BlockSpec(memory_space=pltpu.VMEM)
    return pl.pallas_call(
        attend_kernel,
        out_shape=jax.ShapeDtypeStruct((rows, width), jnp.bfloat16),
        in_specs=[smem] * 4 + [vmem] * 5 + [pl.BlockSpec(memory_space=pl.ANY)],
        out_specs=vmem,
        scratch_shapes=[
            pltpu.VMEM((peers, 2 * WINDOW, heads * 128), jnp.bfloat16),
            pltpu.VMEM((heads, 4, 2 * WINDOW, 128), jnp.bfloat16),
            pltpu.VMEM((rows, width), jnp.float32),
            pltpu.SemaphoreType.DMA((peers, 2)),
        ],
        compiler_params=pltpu.CompilerParams(vmem_limit_bytes=44 * 2**20),
        cost_estimate=pl.CostEstimate(
            flops=rows * width * 2 * WINDOW * 8, bytes_accessed=rows * width * 12,
            transcendentals=rows * width * 4,
        ),
    )(home, offsets, starts, lengths, queries, paired, cosine, sine, sinks, prefix)


def swap(values):
    return lax.ppermute(values, "tp", [(0, 1), (1, 0)])


def local(
    suffix_tokens,
    route_lengths,
    dest_perm,
    attach_points,
    prefix_cache,
    block_of_slot,
    sink_logits,
    attn_gain,
    w_query,
    w_keyval,
    w_out,
    mlp_gain,
    w_gate,
    w_up,
    w_down,
):
    peers = lax.axis_size("req")
    splits = lax.axis_size("tp")
    request_index = lax.axis_index("req")
    tensor_index = lax.axis_index("tp")
    slot_count, slot_length, features = suffix_tokens.shape
    feature_share = features // splits
    slot_share = slot_length // splits
    value_heads = w_keyval.shape[1]
    head_dim = w_keyval.shape[2] // 2
    half_dim = head_dim // 2
    group_tiles = w_query.shape[1] // 128 // value_heads
    row_total = (CAP + (ALIGN - 1) * (peers - 1)) // ALIGN * ALIGN - ALIGN + CHUNK
    peer_ids = jnp.arange(peers)
    slot_steps = jnp.arange(slot_length)
    my_row = lax.dynamic_index_in_dim(dest_perm, request_index, 0, keepdims=False)
    attach_table = attach_points.reshape(peers, peers)
    arriving_lengths = lax.dynamic_index_in_dim(route_lengths, request_index, 0, keepdims=False)
    arriving = (dest_perm == request_index).astype(jnp.int32)
    arriving_attach = jnp.sum(attach_table * arriving, axis=1)
    send_order = jnp.sum(
        jnp.where(my_row[None, :] == peer_ids[:, None], peer_ids[None, :], 0), axis=1
    )
    padded = (arriving_lengths + ALIGN - 1) // ALIGN * ALIGN
    run_ends = jnp.cumsum(padded)
    starts = run_ends - padded
    packed_ids = jnp.arange(row_total)
    source_of = jnp.sum((run_ends[None, :] <= packed_ids[:, None]).astype(jnp.int32), axis=1)
    source_of = jnp.minimum(source_of, peers - 1)
    source_hot = (source_of[:, None] == peer_ids[None, :]).astype(jnp.int32)
    token_index = packed_ids - jnp.sum(source_hot * starts[None, :], axis=1)
    token_index = jnp.minimum(token_index, slot_length - 1)
    positions = jnp.sum(source_hot * arriving_attach[None, :], axis=1) + token_index
    slot_source = jnp.clip(starts[:, None] + slot_steps[None, :], 0, row_total - 1).reshape(-1)
    live_mask = slot_steps[None, :] < arriving_lengths[:, None]

    block_len = prefix_cache.shape[1]
    shelf = prefix_cache.reshape(prefix_cache.shape[0], block_len, -1)
    catalog = jnp.arange(block_of_slot.shape[0])
    home_row = jnp.sum(
        jnp.where(block_of_slot[None, :] == catalog[:, None], catalog[None, :], 0), axis=1
    )
    begin = arriving_attach - WINDOW
    first_block = begin // block_len
    offsets = begin - first_block * block_len
    wanted = jnp.minimum(first_block[:, None] + jnp.arange(2), catalog.shape[0] - 1)
    home = jnp.sum(jnp.where(wanted[..., None] == catalog, home_row, 0), axis=-1)

    share = lax.dynamic_slice_in_dim(suffix_tokens, tensor_index * slot_share, slot_share, 1)
    landed = lax.all_to_all(share[send_order], "req", split_axis=0, concat_axis=0, tiled=True)
    landed, shelf = lax.optimization_barrier((landed, shelf))
    prefix = lax.all_gather(shelf, "req", axis=0, tiled=True)
    part = token_index // slot_share
    within = source_of * slot_share + token_index - part * slot_share
    landed = landed.reshape(peers * slot_share, features)
    if splits == 2:
        mine = landed[within]
        input_rows = jnp.where((part == tensor_index)[:, None], mine, swap(mine))
    else:
        spread = lax.all_gather(landed, "tp", axis=0, tiled=True)
        input_rows = spread[part * (peers * slot_share) + within]
    normed_in = norm_rows(input_rows, attn_gain)
    queries = jnp.dot(normed_in, w_query, preferred_element_type=jnp.float32)
    paired = jnp.dot(
        normed_in, w_keyval.reshape(features, -1), preferred_element_type=jnp.float32
    )
    frequency = ROPE_BASE ** (-(jnp.arange(half_dim).astype(jnp.float32) * 2.0 / head_dim))
    angles = positions.astype(jnp.float32)[:, None] * frequency
    cosine = jnp.tile(jnp.cos(angles), (1, 128 // half_dim))
    sine = jnp.sin(angles)
    sine = jnp.tile(jnp.concatenate([-sine, sine], axis=1), (1, 128 // head_dim))
    sinks = jnp.repeat(sink_logits.reshape(value_heads, group_tiles, 2), CHUNK, axis=1)
    prefix, queries = lax.optimization_barrier((prefix, queries))
    attended = attend(
        queries, paired, cosine, sine, sinks, prefix, home, offsets, starts, arriving_lengths
    )
    partial_value = jnp.dot(attended, w_out, preferred_element_type=jnp.float32).astype(jnp.bfloat16)
    if splits == 2:
        summed = partial_value.astype(jnp.float32) + swap(partial_value).astype(jnp.float32)
    else:
        summed = lax.psum(partial_value, "tp").astype(jnp.float32)
    residual = (input_rows.astype(jnp.float32) + summed).astype(jnp.bfloat16)
    normed_mid = norm_rows(residual, mlp_gain)
    residual_part = lax.dynamic_slice_in_dim(
        residual, tensor_index * feature_share, feature_share, 1
    )
    gate_proj = jnp.dot(normed_mid, w_gate, preferred_element_type=jnp.float32)
    up_proj = jnp.dot(normed_mid, w_up, preferred_element_type=jnp.float32)
    hidden = (jax.nn.silu(gate_proj) * up_proj).astype(jnp.bfloat16)
    down = jnp.dot(hidden, w_down, preferred_element_type=jnp.float32).astype(jnp.bfloat16)
    if splits == 2:
        left, right = down[:, :feature_share], down[:, feature_share:]
        kept = jnp.where(tensor_index == 0, left, right)
        given = swap(jnp.where(tensor_index == 0, right, left))
        down_sum = kept.astype(jnp.float32) + given.astype(jnp.float32)
    else:
        down_sum = lax.psum_scatter(down, "tp", scatter_dimension=1, tiled=True).astype(jnp.float32)
    out_rows = (residual_part.astype(jnp.float32) + down_sum).astype(jnp.bfloat16)
    out_slots = out_rows[slot_source].reshape(peers, slot_length, feature_share)
    out_slots = jnp.where(live_mask[..., None], out_slots, jnp.zeros((), jnp.bfloat16))
    returned = lax.all_to_all(out_slots, "req", split_axis=0, concat_axis=0, tiled=True)
    return returned[my_row]


def solution(mesh):
    in_specs = (
        P("req", None, None),
        P(),
        P(),
        P(),
        P("req", None, "tp", None),
        P(),
        P("tp"),
        P(),
        P(None, "tp"),
        P(None, "tp", None),
        P("tp", None),
        P(),
        P(None, "tp"),
        P(None, "tp"),
        P("tp", None),
    )
    out_specs = P("req", None, "tp")
    return jax.shard_map(local, mesh=mesh, in_specs=in_specs, out_specs=out_specs, check_vma=False)
```

time: 882 us -> 597 us (0.68)
  waiting for transfers between devices: 451 us -> 313 us
  local copies, waits for them, and re-layouts: 184 us -> 54.9 us
  Pallas kernels: 0 us -> 81.9 us
  matrix products: 142 us -> 72.6 us
  other arithmetic: 65.6 us -> 32.9 us
    all_gather x1, waiting for transfers between devices: 281 us -> 50.6 us  [local(): prefix = lax.all_gather(shelf, 'req', axis=0, tiled=True)]
    all_to_all x1, waiting for transfers between devices: 0.01 us -> 118 us  [local(): lax.all_to_all(share[send_order], 'req', split_axis=0, concat_axis=0, til...]
    pallas_call x0 -> x1, Pallas kernels: none -> 81.9 us  [attend(): pl.pallas_call(attend_kernel, out_shape=jax.ShapeDtypeStruct((rows, width...]
    reshape x5 -> x2, local copies, waits for them, and re-layouts: 48.1 us -> 1.07 us  [the longest x1 0.98 us: local(): shelf = prefix_cache.reshape(prefix_cache.shape[0], block_len, -1)]
    gather x9 -> x4, local copies, waits for them, and re-layouts: 78.5 us -> 35.6 us  [the longest x2 22.5 us: local(): mine = landed[within]]
    dot_general x4 -> x3, matrix products: 88.6 us -> 45.8 us  [the longest x1 17.3 us: local(): queries = jnp.dot(normed_in, w_query, preferred_element_type=jnp.float32)]
    psum x1 -> x0, waiting for transfers between devices: 31.4 us -> none  [local(): lax.psum(partial_value.astype(jnp.bfloat16), 'tp').astype(jnp.float32)]
    dot_general x1, matrix products: 35.7 us -> 9.91 us  [local(): jnp.dot(hidden, w_down, preferred_element_type=jnp.float32)]
  transfers between devices with their start and end apart: 5 -> 6, of which waited for: 4 -> 6; matrix products, arithmetic and copies ran while one was open for 4% -> 9% of each run, Pallas kernels for 0% -> 0%
where the time goes in v1:
time: 597 us; the launch traced here: 588 us
  waiting for transfers between devices  313 us (52%)
  Pallas kernels  81.9 us (14%)
  matrix products  72.6 us (12%)
  local copies, waits for them, and re-layouts  54.9 us (9%)
  other arithmetic  32.9 us (6%)
  starting transfers between devices  18.2 us (3%)
  between operations  14.2 us (2%)
    all_to_all x1, waiting for transfers between devices, local(): lax.all_to_all(out_slots, 'req', split_axis=0, concat_axis=0, tiled=True)  124 us
    all_to_all x1, waiting for transfers between devices, local(): lax.all_to_all(share[send_order], 'req', split_axis=0, concat_axis=0, til...  118 us
    pallas_call x1, Pallas kernels, attend(): pl.pallas_call(attend_kernel, out_shape=jax.ShapeDtypeStruct((rows, width...  81.9 us
    all_gather x1, waiting for transfers between devices, local(): prefix = lax.all_gather(shelf, 'req', axis=0, tiled=True)  50.6 us
    gather x2, local copies, waits for them, and re-layouts, local(): mine = landed[within]  22.5 us
    ppermute x3, waiting for transfers between devices, swap(): return lax.ppermute(values, 'tp', [(0, 1), (1, 0)])  20.8 us
    dot_general x1, matrix products, local(): queries = jnp.dot(normed_in, w_query, preferred_element_type=jnp.float32)  17.3 us
    reduce_sum x2, other arithmetic, norm_rows(): jnp.mean(widened * widened, axis=-1, keepdims=True) + EPSILON  16.4 us
  transfers between devices with their start and end apart: 6, of which 6 were waited for; matrix products, arithmetic and copies ran while one was open for 9% of the time, Pallas kernels for 0%

profile of v1, /device:TPU:14, one launch (start us, length us, event | category | flops | bytes accessed | tf_op | source)
XLA Modules:
  0.0 588.0 jit_solution(2346904619666735462)
XLA Ops:
  6.5 0.7 fusion.27
  7.2 0.1 select_reduce_fusion.5
  7.4 5.2 constant_dynamic-slice_fusion.1
  12.6 6.0 %gather_fusion = bf16[16,56,2880]{2,1,0:T(8,128)(2,1)} fusion(bf16[16,56,2880]{2,1,0:T(8,128)(2,1)} %constant_dynamic-slice_fusion.1, s32[1024]{0:T(1024)S(1)} %pad_clamp_fusion.3), kind=kCustom, calls=%fused_computation | custom fusion | bytes 10321984 | tf_op jit(solution)/shard_map/gather | solution.py:227
  18.6 7.3 %all-to-all-start = ((bf16[16,56,2880]{2,1,0:T(8,128)(2,1)}), bf16[16,56,2880]{2,1,0:T(8,128)(2,1)}, u32[]{:S(2)}, u32[]{:S(2)}) async-start(bf16[16,56,2880]{2,1,0:T(8,128)(2,1)} %gather_fusion), calls=%async_computation | async-start | bytes 10551296 | tf_op jit(solution)/shard_map/all_to_all | solution.py:227
  25.9 1.0 reshape.382
  26.9 117.8 %all-to-all-done = bf16[16,56,2880]{2,1,0:T(8,128)(2,1)} async-done(((bf16[16,56,2880]{2,1,0:T(8,128)(2,1)}), bf16[16,56,2880]{2,1,0:T(8,128)(2,1)}, u32[]{:S(2)}, u32[]{:S(2)}) %all-to-all-start) | async-done | bytes 5160992 | tf_op jit(solution)/shard_map/all_to_all | solution.py:227
  144.7 0.7 fusion.26
  145.4 0.1 copy.32
  145.5 0.1 reduce
  145.6 0.1 reshape.384
  145.7 0.1 select_reduce_fusion.4
  145.8 0.1 convert_reduce_fusion
  145.9 0.1 select_reduce_fusion
  146.1 14.7 %gather_fusion.1 = bf16[896,2880]{1,0:T(8,128)(2,1)} fusion(bf16[896,2880]{1,0:T(8,128)(2,1)} %bitcast.6, s32[1024]{0:T(1024)S(1)} %pad_clamp_fusion.2), kind=kCustom, calls=%fused_computation.1 | custom fusion | bytes 10325504 | tf_op jit(solution)/shard_map/gather | solution.py:234
  160.8 7.8 %copy.34 = bf16[896,2880]{0,1:T(8,128)(2,1)} copy(bf16[896,2880]{1,0:T(8,128)(2,1)} %gather_fusion.1) | data formatting | bytes 10321920 | tf_op jit(solution)/shard_map/gather | solution.py:234
  168.7 0.5 fusion.18
  169.2 0.2 copy.37.sine_ref
  169.5 0.2 copy.36.cosine_ref
  169.7 0.1 select_reduce_fusion.2
  169.8 0.2 select_reduce_fusion.3
  170.0 0.1 copy.35.home_ref
  170.1 0.1 reshape.386
  170.2 7.3 %collective-permute-done = bf16[896,2880]{0,1:T(8,128)(2,1)} collective-permute-done((bf16[896,2880]{0,1:T(8,128)(2,1)}, bf16[896,2880]{0,1:T(8,128)(2,1)}, u32[]{:S(2)}, u32[]{:S(2)}) %collective-permute-start) | collective-permute-done | bytes 5160992 | tf_op jit(solution)/shard_map/ppermute | solution.py:159
  177.5 6.1 %fusion.3 = (f32[896]{0:T(1024)S(1)}, bf16[896,2880]{0,1:T(8,128)(2,1)S(1)}) fusion(bf16[896,2880]{0,1:T(8,128)(2,1)} %copy.34, bf16[896,2880]{0,1:T(8,128)(2,1)} %collective-permute-done, pred[896]{0:T(1024)(128)(4,1)S(1)} %fusion.20), kind=kLoop, calls=%fused_computation.12 | loop fusion | flops 10321024 | bytes 15487360 | tf_op jit(solution)/shard_map/reduce_sum | solution.py:18
  183.7 3.3 fusion.7.paired_ref
  187.0 17.3 %fusion.16.query_ref = f32[896,2048]{1,0:T(8,128)} fusion(bf16[2880,2048]{1,0:T(8,128)(2,1)} %param.23, bf16[896,2880]{0,1:T(8,128)(2,1)S(1)} %get-tuple-element.18, f32[2880]{0:T(1024)S(1)} %convert_element_type.70, f32[896]{0:T(1024)S(1)} %add_rsqrt_fusion.1), kind=kOutput, calls=%fused_computation.28 | convolution fusion | flops 10579968000 | bytes 24312576 | tf_op jit(solution)/shard_map/dot_general | solution.py:240
  204.3 50.6 %all-gather.2.cloned.1.call-done.prefix_ref = bf16[64,128,512]{2,1,0:T(8,128)(2,1)} async-done(((bf16[4,128,512]{2,1,0:T(8,128)(2,1)}), bf16[64,128,512]{2,1,0:T(8,128)(2,1)}) %all-gather.2.cloned.1.call-update) | async-done | bytes 8388624 | tf_op jit(solution)/shard_map/all_gather | solution.py:229
  255.0 81.9 %shard_map.145 = bf16[896,2048]{1,0:T(8,128)(2,1)S(1)} custom-call(s32[16,2]{1,0:T(8,128)S(1)} %copy.35.home_ref, s32[16]{0:T(128)S(1)} %get-tuple-element.19.offset_ref, s32[16]{0:T(128)S(1)} %multiply_subtract_fusion.start_ref, s32[16]{0:T(128)S(1)} %bitcast.49, f32[896,2048]{1,0:T(8,128)} %fusion.16.query_ref, f32[896,512]{1,0:T(8,128)S(1)} %fusion.7.paired_ref, ...), custom_call_target="tpu_custom_call" | custom-call | flops 3758096384 | bytes 22020096 | tf_op jit(solution)/shard_map/pallas_call | solution.py:139
  336.9 16.3 %convolution_convert_fusion.1 = bf16[896,2880]{0,1:T(8,128)(2,1)} fusion(bf16[896,2048]{1,0:T(8,128)(2,1)S(1)} %shard_map.145, bf16[2048,2880]{0,1:T(8,128)(2,1)} %param.25), kind=kOutput, calls=%fused_computation.18 | convolution fusion | flops 10572226560 | bytes 20627456 | tf_op jit(solution)/shard_map/dot_general | solution.py:254
  353.4 8.8 %collective-permute-done.1 = bf16[896,2880]{0,1:T(8,128)(2,1)} collective-permute-done((bf16[896,2880]{0,1:T(8,128)(2,1)}, bf16[896,2880]{0,1:T(8,128)(2,1)}, u32[]{:S(2)}, u32[]{:S(2)}) %collective-permute-start.1) | collective-permute-done | bytes 5160992 | tf_op jit(solution)/shard_map/ppermute | solution.py:159
  362.2 10.3 %fusion = (f32[896]{0:T(1024)S(1)}, bf16[896,2880]{0,1:T(8,128)(2,1)}) fusion(bf16[896,2880]{0,1:T(8,128)(2,1)} %collective-permute-done.1, bf16[896,2880]{0,1:T(8,128)(2,1)} %convolution_convert_fusion.1, bf16[896,2880]{0,1:T(8,128)(2,1)} %copy-done.1), kind=kLoop, calls=%fused_computation.9 | loop fusion | flops 23223424 | bytes 20647424 | tf_op jit(solution)/shard_map/reduce_sum | solution.py:18
  372.6 13.5 %fusion.11 = f32[896,1440]{0,1:T(8,128)S(1)} fusion(bf16[2880,1440]{0,1:T(8,128)(2,1)} %param.27, bf16[896,2880]{0,1:T(8,128)(2,1)} %get-tuple-element.16, f32[2880]{0:T(1024)S(1)} %convert_element_type.80, f32[896]{0:T(1024)S(1)} %add_rsqrt_fusion), kind=kOutput, calls=%fused_computation.27 | convolution fusion | flops 7442104320 | bytes 18631424 | tf_op jit(solution)/shard_map/dot_general | solution.py:264
  386.1 12.2 %multiply_convert_fusion.clone.4 = bf16[896,1440]{0,1:T(8,128)(2,1)S(1)} fusion(f32[896,1440]{0,1:T(8,128)S(1)} %fusion.11, bf16[2880,1440]{0,1:T(8,128)(2,1)} %param.28, bf16[896,2880]{0,1:T(8,128)(2,1)S(1)} %copy-done.2, f32[2880]{0:T(1024)S(1)} %convert_element_type.80, f32[896]{0:T(1024)S(1)} %add_rsqrt_fusion), kind=kOutput, calls=%fused_computation.20.clone.clone.clone.1 | convolution fusion | flops 7449845760 | bytes 21211904 | tf_op jit(solution)/shard_map/dot_general | solution.py:265
  398.3 9.9 %convolution_convert_fusion = bf16[896,2880]{0,1:T(8,128)(2,1)S(1)} fusion(bf16[1440,2880]{1,0:T(8,128)(2,1)S(1)} %bitcast.55, bf16[896,1440]{0,1:T(8,128)(2,1)S(1)} %multiply_convert_fusion.clone.4), kind=kOutput, calls=%fused_computation.17 | convolution fusion | flops 7434362880 | bytes 16035840 | tf_op jit(solution)/shard_map/dot_general | solution.py:267
  408.3 2.3 copy-done
  410.5 1.8 broadcast_select_fusion.2
  412.3 0.1 collective-permute-start.2
  412.5 0.1 min.70
  412.7 4.7 collective-permute-done.2
  417.4 6.1 %add_convert_fusion = bf16[896,1440]{0,1:T(8,128)(2,1)} fusion(bf16[896,1440]{0,1:T(8,128)(2,1)S(1)} %collective-permute-done.2, bf16[896,2880]{0,1:T(8,128)(2,1)} %get-tuple-element.16, s32[]{:T(128)S(6)} %select_n.141, pred[]{:T(512)S(6)} %eq.91, bf16[896,2880]{0,1:T(8,128)(2,1)} %copy-done), kind=kLoop, calls=%fused_computation.19 | loop fusion | flops 9031680 | bytes 12902405 | tf_op jit(solution)/shard_map/convert_element_type | solution.py:275
  423.5 3.3 copy.38
  426.7 7.1 %gather_fusion.2 = bf16[1792,1440]{1,0:T(8,128)(2,1)} fusion(bf16[896,1440]{1,0:T(8,128)(2,1)S(1)} %copy.38, s32[2048]{0:T(1024)S(1)} %pad_clamp_fusion), kind=kCustom, calls=%fused_computation.2 | custom fusion | bytes 10329088 | tf_op jit(solution)/shard_map/gather | solution.py:276
  433.8 5.5 broadcast_select_fusion
  439.3 10.6 %all-to-all-start.1 = ((bf16[16,112,1440]{2,1,0:T(8,128)(2,1)}), bf16[16,112,1440]{2,1,0:T(8,128)(2,1)}, u32[]{:S(2)}, u32[]{:S(2)}) async-start(bf16[16,112,1440]{2,1,0:T(8,128)(2,1)} %broadcast_select_fusion), calls=%async_computation.1 | async-start | bytes 11010048 | tf_op jit(solution)/shard_map/all_to_all | solution.py:278
  449.9 0.7 fusion.24
  450.6 124.2 %all-to-all-done.1 = bf16[16,112,1440]{2,1,0:T(8,128)(2,1)} async-done(((bf16[16,112,1440]{2,1,0:T(8,128)(2,1)}), bf16[16,112,1440]{2,1,0:T(8,128)(2,1)}, u32[]{:S(2)}, u32[]{:S(2)}) %all-to-all-start.1) | async-done | bytes 5160992 | tf_op jit(solution)/shard_map/all_to_all | solution.py:278
  574.9 5.9 %gather_fusion.3 = bf16[16,112,1440]{2,1,0:T(8,128)(2,1)} fusion(bf16[16,112,1440]{2,1,0:T(8,128)(2,1)} %all-to-all-done.1, s32[1024]{0:T(1024)S(1)} %pad_clamp_fusion.1), kind=kCustom, calls=%fused_computation.3 | custom fusion | bytes 10321984 | tf_op jit(solution)/shard_map/gather | solution.py:279
  (58 shorter events, 0.7 us)
Async XLA Ops:
  18.6 7.3 %copy-start.3 = (bf16[4,128,4,128]{3,2,1,0:T(4,128)(2,1)S(1)}, bf16[4,128,4,128]{3,2,1,0:T(4,128)(2,1)}, u32[]{:S(2)}) copy-start(bf16[4,128,4,128]{3,2,1,0:T(4,128)(2,1)} %param.19) | copy-start | bytes 1572868
  18.6 127.0 %copy-start.7 = (s32[256]{0:T(256)S(1)}, s32[256]{0:T(256)}, u32[]{:S(2)}) copy-start(s32[256]{0:T(256)} %param.18) | copy-start | bytes 3076
  18.6 127.1 %copy-start.4 = (s32[16,16]{1,0:T(8,128)S(1)}, s32[16,16]{1,0:T(8,128)}, u32[]{:S(2)}) copy-start(s32[16,16]{1,0:T(8,128)} %param.17) | copy-start | bytes 3076
  18.6 126.1 %all-to-all-start = ((bf16[16,56,2880]{2,1,0:T(8,128)(2,1)}), bf16[16,56,2880]{2,1,0:T(8,128)(2,1)}, u32[]{:S(2)}, u32[]{:S(2)}) async-start(bf16[16,56,2880]{2,1,0:T(8,128)(2,1)} %gather_fusion), calls=%async_computation | async-start | bytes 10551296 | tf_op jit(solution)/shard_map/all_to_all | solution.py:227
  25.8 229.1 %all-gather.2.cloned.1.call-start = ((), (), s32[]{:S(2)}) async-start(), calls=%async_computation.2 | async-start | bytes 8912896 | tf_op jit(solution)/shard_map/all_gather | solution.py:229
  160.8 7.8 %copy-start.5 = (bf16[2880]{0:T(1024)(128)(2,1)S(1)}, bf16[2880]{0:T(1024)(128)(2,1)}, u32[]{:S(2)}) copy-start(bf16[2880]{0:T(1024)(128)(2,1)} %param.22) | copy-start | bytes 17284
  160.8 8.8 %copy-start.10 = (s32[64]{0:T(128)S(1)}, s32[64]{0:T(128)}, u32[]{:S(2)}) copy-start(s32[64]{0:T(128)} %param.20) | copy-start | bytes 772
  160.8 9.2 %copy-start.8 = (f32[32]{0:T(128)S(1)}, f32[32]{0:T(128)}, u32[]{:S(2)}) copy-start(f32[32]{0:T(128)} %param.21) | copy-start | bytes 388
  168.6 8.9 %collective-permute-start = (bf16[896,2880]{0,1:T(8,128)(2,1)}, bf16[896,2880]{0,1:T(8,128)(2,1)}, u32[]{:S(2)}, u32[]{:S(2)}) collective-permute-start(bf16[896,2880]{0,1:T(8,128)(2,1)} %copy.34), channel_id=1, source_target_pairs={{0,1},{1,0},{2,3},{3,2},{4,5},{5,4},{6,7},{7,6},{8,9},{9,8},{10,11... | collective-permute-start | bytes 15482888 | tf_op jit(solution)/shard_map/ppermute | solution.py:159
  170.2 13.4 %copy-start.9 = (bf16[2880,4,128]{2,1,0:T(4,128)(2,1)S(1)}, bf16[2880,4,128]{2,1,0:T(4,128)(2,1)}, u32[]{:S(2)}) copy-start(bf16[2880,4,128]{2,1,0:T(4,128)(2,1)} %param.24) | copy-start | bytes 8847364
  183.6 3.4 copy-start.1
  336.9 16.4 %copy-start.6 = (bf16[2880]{0:T(1024)(128)(2,1)S(1)}, bf16[2880]{0:T(1024)(128)(2,1)}, u32[]{:S(2)}) copy-start(bf16[2880]{0:T(1024)(128)(2,1)} %param.26) | copy-start | bytes 17284
  353.3 8.9 %collective-permute-start.1 = (bf16[896,2880]{0,1:T(8,128)(2,1)}, bf16[896,2880]{0,1:T(8,128)(2,1)}, u32[]{:S(2)}, u32[]{:S(2)}) collective-permute-start(bf16[896,2880]{0,1:T(8,128)(2,1)} %convolution_convert_fusion.1), channel_id=1, source_target_pairs={{0,1},{1,0},{2,3},{3,2},{4,5},{5,4},{6,7},{7,6},{8,9},{9,8},{10,11... | collective-permute-start | bytes 15482888 | tf_op jit(solution)/shard_map/ppermute | solution.py:159
  372.5 13.6 %copy-start.2 = (bf16[896,2880]{0,1:T(8,128)(2,1)S(1)}, bf16[896,2880]{0,1:T(8,128)(2,1)}, u32[]{:S(2)}) copy-start(bf16[896,2880]{0,1:T(8,128)(2,1)} %get-tuple-element.16) | copy-start | bytes 15482884
  372.5 25.8 %slice-start = ((s8[8478720]{0:T(1024)(128)(4,1)}), s8[4194304]{0:T(1024)(128)(4,1)S(1)}, s32[]{:S(2)}) async-start(s8[8478720]{0:T(1024)(128)(4,1)} %bitcast.54), calls=%async_computation.3 | async-start | bytes 8388608
  372.5 25.8 %slice-start.1 = ((s8[8478720]{0:T(1024)(128)(4,1)}), s8[4194304]{0:T(1024)(128)(4,1)S(1)}, s32[]{:S(2)}) async-start(s8[8478720]{0:T(1024)(128)(4,1)} %bitcast.54), calls=%async_computation.4 | async-start | bytes 8388608
  386.1 12.2 %slice-start.2 = ((s8[8478720]{0:T(1024)(128)(4,1)}), s8[90112]{0:T(1024)(128)(4,1)S(1)}, s32[]{:S(2)}) async-start(s8[8478720]{0:T(1024)(128)(4,1)} %bitcast.54), calls=%async_computation.5 | async-start | bytes 180224
  408.3 2.3 copy-start
  412.3 5.1 collective-permute-start.2
  439.3 135.6 %all-to-all-start.1 = ((bf16[16,112,1440]{2,1,0:T(8,128)(2,1)}), bf16[16,112,1440]{2,1,0:T(8,128)(2,1)}, u32[]{:S(2)}, u32[]{:S(2)}) async-start(bf16[16,112,1440]{2,1,0:T(8,128)(2,1)} %broadcast_select_fusion), calls=%async_computation.1 | async-start | bytes 11010048 | tf_op jit(solution)/shard_map/all_to_all | solution.py:278
Sparse Core Ops, SparseCore 0:
  144.8 110.1 all-gather.1

commit v2 on v1

--- a/solution.py
+++ b/solution.py
@@ -109,8 +109,10 @@
                     largest = jnp.maximum(jnp.max(score, axis=1, keepdims=True), sink)
                     weight = jnp.exp(score - largest)
                     total = jnp.sum(weight, axis=1, keepdims=True) + jnp.exp(sink - largest)
-                    weight = (weight * (1.0 / total)).astype(jnp.bfloat16)
-                    piece = jnp.dot(weight, tables[k, 2 + side], preferred_element_type=jnp.float32)
+                    piece = jnp.dot(
+                        weight.astype(jnp.bfloat16), tables[k, 2 + side],
+                        preferred_element_type=jnp.float32,
+                    ) * (1.0 / total)
                     result = piece if result is None else result + piece
                 for g in range(group_tiles):
                     at = (k * group_tiles + g) * 128
@@ -153,6 +155,91 @@
             transcendentals=rows * width * 4,
         ),
     )(home, offsets, starts, lengths, queries, paired, cosine, sine, sinks, prefix)
+
+
+def pack_kernel(start_ref, core_ref, mine_ref, other_ref, gain_ref, rows_ref, normed_ref, held):
+    n = pl.program_id(0)
+    share = mine_ref.shape[1]
+    start = pl.multiple_of(start_ref[n], ALIGN)
+    near = pl.multiple_of(start + core_ref[0] * share, ALIGN)
+    far = pl.multiple_of(start + (1 - core_ref[0]) * share, ALIGN)
+
+    @pl.when(n == 0)
+    def _():
+        def clear(i, carry):
+            at = pl.multiple_of(i * ALIGN, ALIGN)
+            held[pl.ds(at, ALIGN), :] = jnp.zeros((ALIGN, held.shape[1]), jnp.float32)
+            return carry
+
+        lax.fori_loop(0, held.shape[0] // ALIGN, clear, 0)
+
+    held[pl.ds(near, share), :] = mine_ref[0].astype(jnp.float32)
+    held[pl.ds(far, share), :] = other_ref[0].astype(jnp.float32)
+
+    @pl.when(n == pl.num_programs(0) - 1)
+    def _():
+        def settle(i, carry):
+            at = pl.multiple_of(i * 16, 16)
+            tile = held[pl.ds(at, 16), :]
+            factor = lax.rsqrt(jnp.mean(tile * tile, axis=1, keepdims=True) + EPSILON)
+            rows_ref[pl.ds(at, 16), :] = tile.astype(jnp.bfloat16)
+            normed_ref[pl.ds(at, 16), :] = (tile * factor * gain_ref[...]).astype(jnp.bfloat16)
+            return carry
+
+        lax.fori_loop(0, rows_ref.shape[0] // 16, settle, 0)
+
+
+def pack(mine, other, starts, tensor_index, gains, row_total):
+    peers, share, features = mine.shape
+    smem = pl.BlockSpec(memory_space=pltpu.SMEM)
+    half = pl.BlockSpec((1, share, features), lambda n: (n, 0, 0))
+    whole = pl.BlockSpec((row_total, features), lambda n: (0, 0))
+    return pl.pallas_call(
+        pack_kernel,
+        grid=(peers,),
+        out_shape=[jax.ShapeDtypeStruct((row_total, features), jnp.bfloat16)] * 2,
+        in_specs=[smem, smem, half, half, pl.BlockSpec((1, features), lambda n: (0, 0))],
+        out_specs=[whole, whole],
+        scratch_shapes=[pltpu.VMEM((row_total + 2 * share, features), jnp.float32)],
+        compiler_params=pltpu.CompilerParams(vmem_limit_bytes=44 * 2**20),
+    )(starts, tensor_index.reshape(1), mine, other, gains.astype(jnp.float32).reshape(1, -1))
+
+
+def unpack_kernel(start_ref, length_ref, residual_ref, kept_ref, given_ref, out_ref, held):
+    n = pl.program_id(0)
+    rows = residual_ref.shape[0]
+    slots, width = out_ref.shape[1:]
+
+    @pl.when(n == 0)
+    def _():
+        def settle(i, carry):
+            at = pl.multiple_of(i * 16, 16)
+            spot = pl.ds(at, 16)
+            moved = kept_ref[spot, :].astype(jnp.float32) + given_ref[spot, :].astype(jnp.float32)
+            held[spot, :] = residual_ref[spot, :].astype(jnp.float32) + moved
+            return carry
+
+        lax.fori_loop(0, rows // 16, settle, 0)
+
+    step = lax.broadcasted_iota(jnp.int32, (slots, width), 0)
+    tile = held[pl.ds(pl.multiple_of(start_ref[n], ALIGN), slots), :]
+    out_ref[0] = jnp.where(step < length_ref[n], tile, 0.0).astype(jnp.bfloat16)
+
+
+def unpack(residual, kept, given, starts, lengths, slot_length):
+    peers = starts.shape[0]
+    rows, width = residual.shape
+    smem = pl.BlockSpec(memory_space=pltpu.SMEM)
+    whole = pl.BlockSpec((rows, width), lambda n: (0, 0))
+    return pl.pallas_call(
+        unpack_kernel,
+        grid=(peers,),
+        out_shape=jax.ShapeDtypeStruct((peers, slot_length, width), jnp.bfloat16),
+        in_specs=[smem, smem, whole, whole, whole],
+        out_specs=pl.BlockSpec((1, slot_length, width), lambda n: (n, 0, 0)),
+        scratch_shapes=[pltpu.VMEM((rows + slot_length, width), jnp.float32)],
+        compiler_params=pltpu.CompilerParams(vmem_limit_bytes=44 * 2**20),
+    )(starts, lengths, residual, kept, given)
 
 
 def swap(values):
@@ -225,18 +312,18 @@
 
     share = lax.dynamic_slice_in_dim(suffix_tokens, tensor_index * slot_share, slot_share, 1)
     landed = lax.all_to_all(share[send_order], "req", split_axis=0, concat_axis=0, tiled=True)
-    landed, shelf = lax.optimization_barrier((landed, shelf))
     prefix = lax.all_gather(shelf, "req", axis=0, tiled=True)
     part = token_index // slot_share
     within = source_of * slot_share + token_index - part * slot_share
-    landed = landed.reshape(peers * slot_share, features)
     if splits == 2:
-        mine = landed[within]
-        input_rows = jnp.where((part == tensor_index)[:, None], mine, swap(mine))
+        input_rows, normed_in = pack(
+            landed, swap(landed), starts, tensor_index, attn_gain, row_total
+        )
     else:
+        landed = landed.reshape(peers * slot_share, features)
         spread = lax.all_gather(landed, "tp", axis=0, tiled=True)
         input_rows = spread[part * (peers * slot_share) + within]
-    normed_in = norm_rows(input_rows, attn_gain)
+        normed_in = norm_rows(input_rows, attn_gain)
     queries = jnp.dot(normed_in, w_query, preferred_element_type=jnp.float32)
     paired = jnp.dot(
         normed_in, w_keyval.reshape(features, -1), preferred_element_type=jnp.float32
@@ -269,12 +356,12 @@
         left, right = down[:, :feature_share], down[:, feature_share:]
         kept = jnp.where(tensor_index == 0, left, right)
         given = swap(jnp.where(tensor_index == 0, right, left))
-        down_sum = kept.astype(jnp.float32) + given.astype(jnp.float32)
+        out_slots = unpack(residual_part, kept, given, starts, arriving_lengths, slot_length)
     else:
         down_sum = lax.psum_scatter(down, "tp", scatter_dimension=1, tiled=True).astype(jnp.float32)
-    out_rows = (residual_part.astype(jnp.float32) + down_sum).astype(jnp.bfloat16)
-    out_slots = out_rows[slot_source].reshape(peers, slot_length, feature_share)
-    out_slots = jnp.where(live_mask[..., None], out_slots, jnp.zeros((), jnp.bfloat16))
+        out_rows = (residual_part.astype(jnp.float32) + down_sum).astype(jnp.bfloat16)
+        out_slots = out_rows[slot_source].reshape(peers, slot_length, feature_share)
+        out_slots = jnp.where(live_mask[..., None], out_slots, jnp.zeros((), jnp.bfloat16))
     returned = lax.all_to_all(out_slots, "req", split_axis=0, concat_axis=0, tiled=True)
     return returned[my_row]
 

time: 597 us -> 646 us (1.082)
  Pallas kernels: 81.9 us -> 128 us
  other arithmetic: 32.9 us -> 18.1 us
  matrix products: 72.6 us -> 82.5 us
  waiting for transfers between devices: 313 us -> 322 us
    all_to_all x1, waiting for transfers between devices: 118 us -> 182 us  [local(): lax.all_to_all(share[send_order], 'req', split_axis=0, concat_axis=0, til...]
    all_gather x1, waiting for transfers between devices: 50.6 us -> 0.01 us  [local(): prefix = lax.all_gather(shelf, 'req', axis=0, tiled=True)]
    gather x3 -> x0, local copies, waits for them, and re-layouts: 29.6 us -> none  [the longest x2 22.5 us: local(): mine = landed[within]]
    pallas_call x0 -> x2, Pallas kernels: none -> 29.2 us  [the longest x1 21.1 us: pack(): pl.pallas_call(pack_kernel, grid=(peers,), out_shape=[jax.ShapeDtypeStruc...]
    dot_general x1, matrix products: 9.91 us -> 29.6 us  [local(): jnp.dot(hidden, w_down, preferred_element_type=jnp.float32)]
    pallas_call x1, Pallas kernels: 81.9 us -> 98.8 us  [attend(): pl.pallas_call(attend_kernel, out_shape=jax.ShapeDtypeStruct((rows, width...]
    ppermute x0 -> x2, local copies, waits for them, and re-layouts: none -> 12.5 us  [swap(): return lax.ppermute(values, 'tp', [(0, 1), (1, 0)])]
    dot_general x1 -> x0, matrix products: 12.2 us -> none  [local(): up_proj = jnp.dot(normed_mid, w_up, preferred_element_type=jnp.float32)]
  transfers between devices with their start and end apart: 6 -> 6, of which waited for: 6 -> 5; matrix products, arithmetic and copies ran while one was open for 9% -> 5% of each run, Pallas kernels for 0% -> 3%
where the time goes in v2:
time: 646 us; the launch traced here: 636 us
  waiting for transfers between devices  322 us (50%)
  Pallas kernels  128 us (20%)
  matrix products  82.5 us (13%)
  local copies, waits for them, and re-layouts  54.4 us (8%)
  other arithmetic  18.1 us (3%)
  starting transfers between devices  16.8 us (3%)
  between operations  13.9 us (2%)
    all_to_all x1, waiting for transfers between devices, local(): lax.all_to_all(share[send_order], 'req', split_axis=0, concat_axis=0, til...  182 us
    all_to_all x1, waiting for transfers between devices, local(): lax.all_to_all(out_slots, 'req', split_axis=0, concat_axis=0, tiled=True)  125 us
    pallas_call x1, Pallas kernels, attend(): pl.pallas_call(attend_kernel, out_shape=jax.ShapeDtypeStruct((rows, width...  98.8 us
    dot_general x1, matrix products, local(): jnp.dot(hidden, w_down, preferred_element_type=jnp.float32)  29.6 us
    pallas_call x1, Pallas kernels, pack(): pl.pallas_call(pack_kernel, grid=(peers,), out_shape=[jax.ShapeDtypeStruc...  21.1 us
    dot_general x1, matrix products, local(): jnp.dot(attended, w_out, preferred_element_type=jnp.float32)  16.3 us
    ppermute x3, waiting for transfers between devices, swap(): return lax.ppermute(values, 'tp', [(0, 1), (1, 0)])  15.3 us
    dot_general x1, matrix products, local(): gate_proj = jnp.dot(normed_mid, w_gate, preferred_element_type=jnp.float32)  15 us
  transfers between devices with their start and end apart: 6, of which 5 were waited for; matrix products, arithmetic and copies ran while one was open for 5% of the time, Pallas kernels for 3%

profile of v2, /device:TPU:14, one launch (start us, length us, event | category | flops | bytes accessed | tf_op | source)
XLA Modules:
  0.0 635.7 jit_solution(953026176226342067)
XLA Ops:
  6.5 0.7 fusion.15
  7.2 0.1 select_reduce_fusion.5
  7.4 5.2 constant_dynamic-slice_fusion.2
  12.6 5.9 gather_fusion
  18.6 7.3 %all-to-all-start = ((bf16[16,56,2880]{2,1,0:T(8,128)(2,1)}), bf16[16,56,2880]{2,1,0:T(8,128)(2,1)}, u32[]{:S(2)}, u32[]{:S(2)}) async-start(bf16[16,56,2880]{2,1,0:T(8,128)(2,1)} %gather_fusion), calls=%async_computation | async-start | bytes 10551296 | tf_op jit(solution)/shard_map/all_to_all | solution.py:314
  25.9 0.0 all-gather.2.cloned.1.call-start
  25.9 1.0 reshape.243
  26.9 181.9 %all-to-all-done.mine_ref = bf16[16,56,2880]{2,1,0:T(8,128)(2,1)} async-done(((bf16[16,56,2880]{2,1,0:T(8,128)(2,1)}), bf16[16,56,2880]{2,1,0:T(8,128)(2,1)}, u32[]{:S(2)}, u32[]{:S(2)}) %all-to-all-start) | async-done | bytes 5160992 | tf_op jit(solution)/shard_map/all_to_all | solution.py:314
  208.9 0.7 fusion.14
  209.6 0.1 copy.33
  209.7 0.1 reduce
  209.8 0.1 reshape.242
  209.9 0.1 select_reduce_fusion.4
  210.0 0.1 convert_reduce_fusion
  210.1 0.1 select_reduce_fusion
  210.2 0.5 fusion.10
  210.8 0.2 copy.36.sine_ref
  211.0 0.2 copy.35.cosine_ref
  211.3 0.1 select_reduce_fusion.2
  211.4 0.2 select_reduce_fusion.3
  211.6 0.1 copy.34.home_ref
  211.7 0.1 reshape.246
  211.8 6.1 collective-permute-done.other_ref
  217.9 21.1 %shard_map.145 = (bf16[896,2880]{1,0:T(8,128)(2,1)S(1)}, bf16[896,2880]{1,0:T(8,128)(2,1)}) custom-call(s32[16]{0:T(128)S(1)} %multiply_subtract_fusion.1.start_ref, s32[1]{0:T(128)} %bitcast.2.core_ref, bf16[16,56,2880]{2,1,0:T(8,128)(2,1)} %all-to-all-done.mine_ref, bf16[16,56,2880]{2,1,0:T(8,128)(2,1)} %collective-permute-done.other_ref, ...), custom_call_target="tpu_custom_call" | custom-call | tf_op jit(solution)/shard_map/pallas_call | solution.py:197
  239.0 7.8 %fusion.3.paired_ref = f32[896,512]{1,0:T(8,128)S(1)} fusion(bf16[896,2880]{1,0:T(8,128)(2,1)} %get-tuple-element.10, bf16[360,8,4,128]{3,2,1,0:T(4,128)(2,1)} %bitcast.51), kind=kOutput, calls=%fused_computation.11 | convolution fusion | flops 2642411520 | bytes 9945088 | tf_op jit(solution)/shard_map/dot_general | solution.py:328
  246.8 1.4 copy-done.9
  248.3 13.7 %fusion.17.query_ref = f32[896,2048]{1,0:T(8,128)} fusion(bf16[896,2880]{1,0:T(8,128)(2,1)S(1)} %copy-done.9, bf16[2880,2048]{1,0:T(8,128)(2,1)S(1)} %bitcast.50), kind=kOutput, calls=%fused_computation.72 | convolution fusion | flops 10569646080 | bytes 24297472 | tf_op jit(solution)/shard_map/dot_general | solution.py:327
  262.0 98.8 %shard_map.146 = bf16[896,2048]{1,0:T(8,128)(2,1)S(1)} custom-call(s32[16,2]{1,0:T(8,128)S(1)} %copy.34.home_ref, s32[16]{0:T(128)S(1)} %get-tuple-element.17.offset_ref, s32[16]{0:T(128)S(1)} %multiply_subtract_fusion.1.start_ref, s32[16]{0:T(128)S(1)} %bitcast.45, f32[896,2048]{1,0:T(8,128)} %fusion.17.query_ref, f32[896,512]{1,0:T(8,128)S(1)} %fusion.3.paired_ref, ...), custom_call_target="tpu_custom_call" | custom-call | flops 3758096384 | bytes 22020096 | tf_op jit(solution)/shard_map/pallas_call | solution.py:141
  360.8 16.3 %convolution_convert_fusion.1 = bf16[896,2880]{1,0:T(8,128)(2,1)} fusion(bf16[896,2048]{1,0:T(8,128)(2,1)S(1)} %shard_map.146, bf16[2048,2880]{0,1:T(8,128)(2,1)} %param.25), kind=kOutput, calls=%fused_computation.9 | convolution fusion | flops 10572226560 | bytes 20627456 | tf_op jit(solution)/shard_map/dot_general | solution.py:341
  377.2 8.0 %copy.38 = bf16[896,2880]{0,1:T(8,128)(2,1)} copy(bf16[896,2880]{1,0:T(8,128)(2,1)} %convolution_convert_fusion.1) | data formatting | bytes 10321920 | tf_op jit(solution)/shard_map/convert_element_type | solution.py:341
  385.2 0.1 collective-permute-start.1
  385.4 8.7 %collective-permute-done.1 = bf16[896,2880]{0,1:T(8,128)(2,1)} collective-permute-done((bf16[896,2880]{0,1:T(8,128)(2,1)}, bf16[896,2880]{0,1:T(8,128)(2,1)}, u32[]{:S(2)}, u32[]{:S(2)}) %collective-permute-start.1) | collective-permute-done | bytes 5160992 | tf_op jit(solution)/shard_map/ppermute | solution.py:246
  394.1 8.1 %copy.39 = bf16[896,2880]{1,0:T(8,128)(2,1)} copy(bf16[896,2880]{0,1:T(8,128)(2,1)} %collective-permute-done.1) | data formatting | bytes 10321920 | tf_op jit(solution)/shard_map/ppermute | solution.py:246
  402.2 10.9 %fusion = (f32[896]{0:T(1024)S(1)}, bf16[896,2880]{1,0:T(8,128)(2,1)}) fusion(bf16[896,2880]{1,0:T(8,128)(2,1)} %copy.39, bf16[896,2880]{1,0:T(8,128)(2,1)} %convolution_convert_fusion.1, bf16[896,2880]{1,0:T(8,128)(2,1)} %copy-done.2), kind=kLoop, calls=%fused_computation.4 | loop fusion | flops 23223424 | bytes 20647424 | tf_op jit(solution)/shard_map/reduce_sum | solution.py:18
  413.2 15.0 %fusion.8 = f32[896,1440]{0,1:T(8,128)} fusion(bf16[2880,1440]{0,1:T(8,128)(2,1)} %param.27, bf16[896,2880]{1,0:T(8,128)(2,1)} %get-tuple-element.16, f32[2880]{0:T(1024)S(1)} %convert_element_type.59, f32[896]{0:T(1024)S(1)} %add_rsqrt_fusion), kind=kOutput, calls=%fused_computation.16 | convolution fusion | flops 7442104320 | bytes 18631424 | tf_op jit(solution)/shard_map/dot_general | solution.py:351
  428.2 29.6 %convolution_convert_fusion = bf16[896,2880]{1,0:T(8,128)(2,1)} fusion(bf16[1440,2880]{1,0:T(8,128)(2,1)} %param.29, f32[896,1440]{0,1:T(8,128)} %fusion.8, bf16[2880,1440]{0,1:T(8,128)(2,1)} %param.28, bf16[896,2880]{1,0:T(8,128)(2,1)} %get-tuple-element.16, f32[2880]{0:T(1024)S(1)} %convert_element_type.59, f32[896]{0:T(1024)S(1)} %add_rsqrt_fusion), kind=kOutput, calls=%fused_computation.8 | convolution fusion | flops 14884208640 | bytes 32086784 | tf_op jit(solution)/shard_map/dot_general | solution.py:354
  457.8 5.0 broadcast_select_fusion
  462.9 4.5 copy.41
  467.4 0.1 collective-permute-start.2
  467.5 4.6 constant_dynamic-slice_fusion.residual_ref
  472.2 0.4 collective-permute-done.2
  472.6 4.4 copy.42.given_ref
  477.0 1.8 copy-done
  478.8 1.8 copy-done.1
  480.6 8.1 %shard_map.147 = bf16[16,112,1440]{2,1,0:T(8,128)(2,1)} custom-call(s32[16]{0:T(128)S(1)} %multiply_subtract_fusion.1.start_ref, s32[16]{0:T(128)S(1)} %bitcast.46, bf16[896,1440]{1,0:T(8,128)(2,1)S(1)} %copy-done, bf16[896,1440]{1,0:T(8,128)(2,1)S(1)} %get-tuple-element.22.kept_ref, bf16[896,1440]{1,0:T(8,128)(2,1)S(1)} %copy-done.1), custom_call_target="tpu_custom_call" | custom-call | tf_op jit(solution)/shard_map/pallas_call | solution.py:234
  488.6 9.2 %all-to-all-start.1 = ((bf16[16,112,1440]{2,1,0:T(8,128)(2,1)}), bf16[16,112,1440]{2,1,0:T(8,128)(2,1)}, u32[]{:S(2)}, u32[]{:S(2)}) async-start(bf16[16,112,1440]{2,1,0:T(8,128)(2,1)} %shard_map.147), calls=%async_computation.1 | async-start | bytes 11010048 | tf_op jit(solution)/shard_map/all_to_all | solution.py:365
  497.8 124.9 %all-to-all-done.1 = bf16[16,112,1440]{2,1,0:T(8,128)(2,1)} async-done(((bf16[16,112,1440]{2,1,0:T(8,128)(2,1)}), bf16[16,112,1440]{2,1,0:T(8,128)(2,1)}, u32[]{:S(2)}, u32[]{:S(2)}) %all-to-all-start.1) | async-done | bytes 5160992 | tf_op jit(solution)/shard_map/all_to_all | solution.py:365
  622.8 5.9 gather_fusion.1
  (48 shorter events, 0.3 us)
Async XLA Ops:
  18.6 7.4 %copy-start.3 = (bf16[4,128,4,128]{3,2,1,0:T(4,128)(2,1)S(1)}, bf16[4,128,4,128]{3,2,1,0:T(4,128)(2,1)}, u32[]{:S(2)}) copy-start(bf16[4,128,4,128]{3,2,1,0:T(4,128)(2,1)} %param.19) | copy-start | bytes 1572868
  18.6 191.3 %copy-start.7 = (s32[256]{0:T(256)S(1)}, s32[256]{0:T(256)}, u32[]{:S(2)}) copy-start(s32[256]{0:T(256)} %param.18) | copy-start | bytes 3076
  18.6 191.3 %copy-start.4 = (s32[16,16]{1,0:T(8,128)S(1)}, s32[16,16]{1,0:T(8,128)}, u32[]{:S(2)}) copy-start(s32[16,16]{1,0:T(8,128)} %param.17) | copy-start | bytes 3076
  18.6 190.3 %all-to-all-start = ((bf16[16,56,2880]{2,1,0:T(8,128)(2,1)}), bf16[16,56,2880]{2,1,0:T(8,128)(2,1)}, u32[]{:S(2)}, u32[]{:S(2)}) async-start(bf16[16,56,2880]{2,1,0:T(8,128)(2,1)} %gather_fusion), calls=%async_computation | async-start | bytes 10551296 | tf_op jit(solution)/shard_map/all_to_all | solution.py:314
  25.8 185.4 %copy-start.5 = (bf16[2880]{0:T(1024)(128)(2,1)S(1)}, bf16[2880]{0:T(1024)(128)(2,1)}, u32[]{:S(2)}) copy-start(bf16[2880]{0:T(1024)(128)(2,1)} %param.22) | copy-start | bytes 17284
  25.8 185.4 %copy-start.10 = (s32[64]{0:T(128)S(1)}, s32[64]{0:T(128)}, u32[]{:S(2)}) copy-start(s32[64]{0:T(128)} %param.20) | copy-start | bytes 772
  25.9 185.8 %copy-start.8 = (f32[32]{0:T(128)S(1)}, f32[32]{0:T(128)}, u32[]{:S(2)}) copy-start(f32[32]{0:T(128)} %param.21) | copy-start | bytes 388
  25.9 236.1 %all-gather.2.cloned.1.call-start = ((), (), s32[]{:S(2)}) async-start(), calls=%async_computation.2 | async-start | bytes 8912896 | tf_op jit(solution)/shard_map/all_gather | solution.py:315
  208.9 9.0 %collective-permute-start = (bf16[16,56,2880]{2,1,0:T(8,128)(2,1)}, bf16[16,56,2880]{2,1,0:T(8,128)(2,1)}, u32[]{:S(2)}, u32[]{:S(2)}) collective-permute-start(bf16[16,56,2880]{2,1,0:T(8,128)(2,1)} %all-to-all-done.mine_ref), channel_id=1, source_target_pairs={{0,1},{1,0},{2,3},{3,2},{4,5},{5,4},{6,7},{7,6},{8,9},{9,8},{10,11... | collective-permute-start | bytes 15482888 | tf_op jit(solution)/shard_map/ppermute | solution.py:246
  217.9 28.9 %slice-start = ((s8[11796480]{0:T(1024)(128)(4,1)}), s8[3407872]{0:T(1024)(128)(4,1)S(1)}, s32[]{:S(2)}) async-start(s8[11796480]{0:T(1024)(128)(4,1)} %bitcast.49), calls=%async_computation.3 | async-start | bytes 6815744
  239.0 7.8 %copy-start.2 = (bf16[896,2880]{1,0:T(8,128)(2,1)}, bf16[896,2880]{1,0:T(8,128)(2,1)S(1)}, u32[]{:S(2)}) copy-start(bf16[896,2880]{1,0:T(8,128)(2,1)S(1)} %get-tuple-element.9) | copy-start | bytes 15482884
  239.0 7.8 %slice-start.1 = ((s8[11796480]{0:T(1024)(128)(4,1)}), s8[4194304]{0:T(1024)(128)(4,1)S(1)}, s32[]{:S(2)}) async-start(s8[11796480]{0:T(1024)(128)(4,1)} %bitcast.49), calls=%async_computation.4 | async-start | bytes 8388608
  239.0 7.8 %slice-start.2 = ((s8[11796480]{0:T(1024)(128)(4,1)}), s8[4194304]{0:T(1024)(128)(4,1)S(1)}, s32[]{:S(2)}) async-start(s8[11796480]{0:T(1024)(128)(4,1)} %bitcast.49), calls=%async_computation.5 | async-start | bytes 8388608
  239.0 9.3 %copy-start.9 = (bf16[896,2880]{1,0:T(8,128)(2,1)S(1)}, bf16[896,2880]{1,0:T(8,128)(2,1)}, u32[]{:S(2)}) copy-start(bf16[896,2880]{1,0:T(8,128)(2,1)} %get-tuple-element.10) | copy-start | bytes 15482884
  377.2 8.2 %copy-start.6 = (bf16[2880]{0:T(1024)(128)(2,1)S(1)}, bf16[2880]{0:T(1024)(128)(2,1)}, u32[]{:S(2)}) copy-start(bf16[2880]{0:T(1024)(128)(2,1)} %param.26) | copy-start | bytes 17284
  385.2 8.9 %collective-permute-start.1 = (bf16[896,2880]{0,1:T(8,128)(2,1)}, bf16[896,2880]{0,1:T(8,128)(2,1)}, u32[]{:S(2)}, u32[]{:S(2)}) collective-permute-start(bf16[896,2880]{0,1:T(8,128)(2,1)} %copy.38), channel_id=1, source_target_pairs={{0,1},{1,0},{2,3},{3,2},{4,5},{5,4},{6,7},{7,6},{8,9},{9,8},{10,11... | collective-permute-start | bytes 15482888 | tf_op jit(solution)/shard_map/ppermute | solution.py:246
  467.4 5.2 collective-permute-start.2
  477.0 1.8 copy-start
  478.8 1.8 copy-start.1
  488.6 134.1 %all-to-all-start.1 = ((bf16[16,112,1440]{2,1,0:T(8,128)(2,1)}), bf16[16,112,1440]{2,1,0:T(8,128)(2,1)}, u32[]{:S(2)}, u32[]{:S(2)}) async-start(bf16[16,112,1440]{2,1,0:T(8,128)(2,1)} %shard_map.147), calls=%async_computation.1 | async-start | bytes 11010048 | tf_op jit(solution)/shard_map/all_to_all | solution.py:365
Sparse Core Ops, SparseCore 0:
  29.5 192.9 all-gather.1

commit v3 on v1

--- a/solution.py
+++ b/solution.py
@@ -225,7 +225,6 @@
 
     share = lax.dynamic_slice_in_dim(suffix_tokens, tensor_index * slot_share, slot_share, 1)
     landed = lax.all_to_all(share[send_order], "req", split_axis=0, concat_axis=0, tiled=True)
-    landed, shelf = lax.optimization_barrier((landed, shelf))
     prefix = lax.all_gather(shelf, "req", axis=0, tiled=True)
     part = token_index // slot_share
     within = source_of * slot_share + token_index - part * slot_share

time: 597 us -> 611 us (1.023)
  waiting for transfers between devices: 313 us -> 325 us
    all_to_all x1, waiting for transfers between devices: 118 us -> 180 us  [local(): lax.all_to_all(share[send_order], 'req', split_axis=0, concat_axis=0, til...]
    all_gather x1, waiting for transfers between devices: 50.6 us -> 0.01 us  [local(): prefix = lax.all_gather(shelf, 'req', axis=0, tiled=True)]
  transfers between devices with their start and end apart: 6 -> 6, of which waited for: 6 -> 5; matrix products, arithmetic and copies ran while one was open for 9% -> 9% of each run, Pallas kernels for 0% -> 0%
where the time goes in v3:
time: 611 us; the launch traced here: 603 us
  waiting for transfers between devices  325 us (53%)
  Pallas kernels  79.8 us (13%)
  matrix products  72.6 us (12%)
  local copies, waits for them, and re-layouts  54.8 us (9%)
  other arithmetic  32.8 us (5%)
  starting transfers between devices  23.9 us (4%)
  between operations  14.2 us (2%)
    all_to_all x1, waiting for transfers between devices, local(): lax.all_to_all(share[send_order], 'req', split_axis=0, concat_axis=0, til...  180 us
    all_to_all x1, waiting for transfers between devices, local(): lax.all_to_all(out_slots, 'req', split_axis=0, concat_axis=0, tiled=True)  124 us
    pallas_call x1, Pallas kernels, attend(): pl.pallas_call(attend_kernel, out_shape=jax.ShapeDtypeStruct((rows, width...  79.8 us
    gather x2, local copies, waits for them, and re-layouts, local(): mine = landed[within]  22.5 us
    ppermute x3, waiting for transfers between devices, swap(): return lax.ppermute(values, 'tp', [(0, 1), (1, 0)])  20.7 us
    dot_general x1, matrix products, local(): queries = jnp.dot(normed_in, w_query, preferred_element_type=jnp.float32)  17.3 us
    reduce_sum x2, other arithmetic, norm_rows(): jnp.mean(widened * widened, axis=-1, keepdims=True) + EPSILON  16.4 us
    dot_general x1, matrix products, local(): jnp.dot(attended, w_out, preferred_element_type=jnp.float32)  16.3 us
  transfers between devices with their start and end apart: 6, of which 5 were waited for; matrix products, arithmetic and copies ran while one was open for 9% of the time, Pallas kernels for 0%

profile of v3, /device:TPU:14, one launch (start us, length us, event | category | flops | bytes accessed | tf_op | source)
XLA Modules:
  0.0 603.4 jit_solution(9067897225164766233)
XLA Ops:
  6.5 0.7 fusion.27
  7.2 0.1 select_reduce_fusion.5
  7.4 5.2 constant_dynamic-slice_fusion.1
  12.6 5.9 gather_fusion
  18.5 7.3 %all-to-all-start = ((bf16[16,56,2880]{2,1,0:T(8,128)(2,1)}), bf16[16,56,2880]{2,1,0:T(8,128)(2,1)}, u32[]{:S(2)}, u32[]{:S(2)}) async-start(bf16[16,56,2880]{2,1,0:T(8,128)(2,1)} %gather_fusion), calls=%async_computation | async-start | bytes 10551296 | tf_op jit(solution)/shard_map/all_to_all | solution.py:227
  25.9 1.0 reshape.384
  26.9 0.7 fusion.26
  27.6 0.1 copy.32
  27.7 0.1 reduce
  27.8 0.1 reshape.383
  27.9 0.1 select_reduce_fusion.4
  28.0 0.1 convert_reduce_fusion
  28.1 0.1 select_reduce_fusion
  28.3 180.4 %all-to-all-done = bf16[16,56,2880]{2,1,0:T(8,128)(2,1)} async-done(((bf16[16,56,2880]{2,1,0:T(8,128)(2,1)}), bf16[16,56,2880]{2,1,0:T(8,128)(2,1)}, u32[]{:S(2)}, u32[]{:S(2)}) %all-to-all-start) | async-done | bytes 5160992 | tf_op jit(solution)/shard_map/all_to_all | solution.py:227
  208.7 14.7 %gather_fusion.1 = bf16[896,2880]{1,0:T(8,128)(2,1)} fusion(bf16[896,2880]{1,0:T(8,128)(2,1)} %bitcast.6, s32[1024]{0:T(1024)S(1)} %pad_clamp_fusion.2), kind=kCustom, calls=%fused_computation.1 | custom fusion | bytes 10325504 | tf_op jit(solution)/shard_map/gather | solution.py:233
  223.4 7.7 %copy.34 = bf16[896,2880]{0,1:T(8,128)(2,1)} copy(bf16[896,2880]{1,0:T(8,128)(2,1)} %gather_fusion.1) | data formatting | bytes 10321920 | tf_op jit(solution)/shard_map/gather | solution.py:233
  231.2 0.5 fusion.18
  231.8 0.2 copy.37.sine_ref
  232.0 0.2 copy.36.cosine_ref
  232.2 0.1 select_reduce_fusion.2
  232.4 0.2 select_reduce_fusion.3
  232.6 0.1 copy.35.home_ref
  232.6 0.1 reshape.386
  232.8 7.3 %collective-permute-done = bf16[896,2880]{0,1:T(8,128)(2,1)} collective-permute-done((bf16[896,2880]{0,1:T(8,128)(2,1)}, bf16[896,2880]{0,1:T(8,128)(2,1)}, u32[]{:S(2)}, u32[]{:S(2)}) %collective-permute-start) | collective-permute-done | bytes 5160992 | tf_op jit(solution)/shard_map/ppermute | solution.py:159
  240.1 6.1 %fusion.3 = (f32[896]{0:T(1024)S(1)}, bf16[896,2880]{0,1:T(8,128)(2,1)S(1)}) fusion(bf16[896,2880]{0,1:T(8,128)(2,1)} %copy.34, bf16[896,2880]{0,1:T(8,128)(2,1)} %collective-permute-done, pred[896]{0:T(1024)(128)(4,1)S(1)} %fusion.20), kind=kLoop, calls=%fused_computation.12 | loop fusion | flops 10321024 | bytes 15487360 | tf_op jit(solution)/shard_map/reduce_sum | solution.py:18
  246.2 3.3 fusion.7.paired_ref
  249.5 17.3 %fusion.16.query_ref = f32[896,2048]{1,0:T(8,128)} fusion(bf16[2880,2048]{1,0:T(8,128)(2,1)} %param.23, bf16[896,2880]{0,1:T(8,128)(2,1)S(1)} %get-tuple-element.14, f32[2880]{0:T(1024)S(1)} %convert_element_type.70, f32[896]{0:T(1024)S(1)} %add_rsqrt_fusion.1), kind=kOutput, calls=%fused_computation.28 | convolution fusion | flops 10579968000 | bytes 24312576 | tf_op jit(solution)/shard_map/dot_general | solution.py:239
  266.8 79.8 %shard_map.145 = bf16[896,2048]{1,0:T(8,128)(2,1)S(1)} custom-call(s32[16,2]{1,0:T(8,128)S(1)} %copy.35.home_ref, s32[16]{0:T(128)S(1)} %get-tuple-element.15.offset_ref, s32[16]{0:T(128)S(1)} %multiply_subtract_fusion.start_ref, s32[16]{0:T(128)S(1)} %bitcast.49, f32[896,2048]{1,0:T(8,128)} %fusion.16.query_ref, f32[896,512]{1,0:T(8,128)S(1)} %fusion.7.paired_ref, ...), custom_call_target="tpu_custom_call" | custom-call | flops 3758096384 | bytes 22020096 | tf_op jit(solution)/shard_map/pallas_call | solution.py:139
  346.6 16.3 %convolution_convert_fusion.1 = bf16[896,2880]{0,1:T(8,128)(2,1)} fusion(bf16[896,2048]{1,0:T(8,128)(2,1)S(1)} %shard_map.145, bf16[2048,2880]{0,1:T(8,128)(2,1)} %param.25), kind=kOutput, calls=%fused_computation.18 | convolution fusion | flops 10572226560 | bytes 20627456 | tf_op jit(solution)/shard_map/dot_general | solution.py:253
  363.0 0.2 collective-permute-start.1
  363.2 8.7 %collective-permute-done.1 = bf16[896,2880]{0,1:T(8,128)(2,1)} collective-permute-done((bf16[896,2880]{0,1:T(8,128)(2,1)}, bf16[896,2880]{0,1:T(8,128)(2,1)}, u32[]{:S(2)}, u32[]{:S(2)}) %collective-permute-start.1) | collective-permute-done | bytes 5160992 | tf_op jit(solution)/shard_map/ppermute | solution.py:159
  371.9 10.3 %fusion = (f32[896]{0:T(1024)S(1)}, bf16[896,2880]{0,1:T(8,128)(2,1)}) fusion(bf16[896,2880]{0,1:T(8,128)(2,1)} %collective-permute-done.1, bf16[896,2880]{0,1:T(8,128)(2,1)} %convolution_convert_fusion.1, bf16[896,2880]{0,1:T(8,128)(2,1)} %copy-done.1), kind=kLoop, calls=%fused_computation.9 | loop fusion | flops 23223424 | bytes 20647424 | tf_op jit(solution)/shard_map/reduce_sum | solution.py:18
  382.3 13.5 %fusion.11 = f32[896,1440]{0,1:T(8,128)S(1)} fusion(bf16[2880,1440]{0,1:T(8,128)(2,1)} %param.27, bf16[896,2880]{0,1:T(8,128)(2,1)} %get-tuple-element.12, f32[2880]{0:T(1024)S(1)} %convert_element_type.80, f32[896]{0:T(1024)S(1)} %add_rsqrt_fusion), kind=kOutput, calls=%fused_computation.27 | convolution fusion | flops 7442104320 | bytes 18631424 | tf_op jit(solution)/shard_map/dot_general | solution.py:263
  395.8 12.2 %multiply_convert_fusion.clone.4 = bf16[896,1440]{0,1:T(8,128)(2,1)S(1)} fusion(f32[896,1440]{0,1:T(8,128)S(1)} %fusion.11, bf16[2880,1440]{0,1:T(8,128)(2,1)} %param.28, bf16[896,2880]{0,1:T(8,128)(2,1)S(1)} %copy-done.2, f32[2880]{0:T(1024)S(1)} %convert_element_type.80, f32[896]{0:T(1024)S(1)} %add_rsqrt_fusion), kind=kOutput, calls=%fused_computation.20.clone.clone.clone.1 | convolution fusion | flops 7449845760 | bytes 21211904 | tf_op jit(solution)/shard_map/dot_general | solution.py:264
  408.1 9.9 %convolution_convert_fusion = bf16[896,2880]{0,1:T(8,128)(2,1)S(1)} fusion(bf16[1440,2880]{1,0:T(8,128)(2,1)S(1)} %bitcast.55, bf16[896,1440]{0,1:T(8,128)(2,1)S(1)} %multiply_convert_fusion.clone.4), kind=kOutput, calls=%fused_computation.17 | convolution fusion | flops 7434362880 | bytes 16035840 | tf_op jit(solution)/shard_map/dot_general | solution.py:266
  418.0 2.3 copy-done
  420.2 1.8 broadcast_select_fusion.2
  422.0 0.1 collective-permute-start.2
  422.2 0.1 min.70
  422.5 4.6 collective-permute-done.2
  427.1 6.1 %add_convert_fusion = bf16[896,1440]{0,1:T(8,128)(2,1)} fusion(bf16[896,1440]{0,1:T(8,128)(2,1)S(1)} %collective-permute-done.2, bf16[896,2880]{0,1:T(8,128)(2,1)} %get-tuple-element.12, s32[]{:T(128)S(6)} %select_n.141, pred[]{:T(512)S(6)} %eq.91, bf16[896,2880]{0,1:T(8,128)(2,1)} %copy-done), kind=kLoop, calls=%fused_computation.19 | loop fusion | flops 9031680 | bytes 12902405 | tf_op jit(solution)/shard_map/convert_element_type | solution.py:274
  433.2 3.3 copy.38
  436.5 7.1 %gather_fusion.2 = bf16[1792,1440]{1,0:T(8,128)(2,1)} fusion(bf16[896,1440]{1,0:T(8,128)(2,1)S(1)} %copy.38, s32[2048]{0:T(1024)S(1)} %pad_clamp_fusion), kind=kCustom, calls=%fused_computation.2 | custom fusion | bytes 10329088 | tf_op jit(solution)/shard_map/gather | solution.py:275
  443.5 5.5 broadcast_select_fusion
  449.0 16.3 %all-to-all-start.1 = ((bf16[16,112,1440]{2,1,0:T(8,128)(2,1)}), bf16[16,112,1440]{2,1,0:T(8,128)(2,1)}, u32[]{:S(2)}, u32[]{:S(2)}) async-start(bf16[16,112,1440]{2,1,0:T(8,128)(2,1)} %broadcast_select_fusion), calls=%async_computation.1 | async-start | bytes 11010048 | tf_op jit(solution)/shard_map/all_to_all | solution.py:277
  465.2 0.7 fusion.24
  465.9 124.3 %all-to-all-done.1 = bf16[16,112,1440]{2,1,0:T(8,128)(2,1)} async-done(((bf16[16,112,1440]{2,1,0:T(8,128)(2,1)}), bf16[16,112,1440]{2,1,0:T(8,128)(2,1)}, u32[]{:S(2)}, u32[]{:S(2)}) %all-to-all-start.1) | async-done | bytes 5160992 | tf_op jit(solution)/shard_map/all_to_all | solution.py:277
  590.3 5.9 gather_fusion.3
  (58 shorter events, 0.6 us)
Async XLA Ops:
  18.5 7.3 %copy-start.3 = (bf16[4,128,4,128]{3,2,1,0:T(4,128)(2,1)S(1)}, bf16[4,128,4,128]{3,2,1,0:T(4,128)(2,1)}, u32[]{:S(2)}) copy-start(bf16[4,128,4,128]{3,2,1,0:T(4,128)(2,1)} %param.19) | copy-start | bytes 1572868
  18.5 9.3 %copy-start.7 = (s32[256]{0:T(256)S(1)}, s32[256]{0:T(256)}, u32[]{:S(2)}) copy-start(s32[256]{0:T(256)} %param.18) | copy-start | bytes 3076
  18.5 9.4 %copy-start.4 = (s32[16,16]{1,0:T(8,128)S(1)}, s32[16,16]{1,0:T(8,128)}, u32[]{:S(2)}) copy-start(s32[16,16]{1,0:T(8,128)} %param.17) | copy-start | bytes 3076
  18.5 190.2 %all-to-all-start = ((bf16[16,56,2880]{2,1,0:T(8,128)(2,1)}), bf16[16,56,2880]{2,1,0:T(8,128)(2,1)}, u32[]{:S(2)}, u32[]{:S(2)}) async-start(bf16[16,56,2880]{2,1,0:T(8,128)(2,1)} %gather_fusion), calls=%async_computation | async-start | bytes 10551296 | tf_op jit(solution)/shard_map/all_to_all | solution.py:227
  25.8 241.0 %all-gather.2.cloned.1.call-start = ((), (), s32[]{:S(2)}) async-start(), calls=%async_computation.2 | async-start | bytes 8912896 | tf_op jit(solution)/shard_map/all_gather | solution.py:228
  223.4 7.8 %copy-start.5 = (bf16[2880]{0:T(1024)(128)(2,1)S(1)}, bf16[2880]{0:T(1024)(128)(2,1)}, u32[]{:S(2)}) copy-start(bf16[2880]{0:T(1024)(128)(2,1)} %param.22) | copy-start | bytes 17284
  223.4 8.8 %copy-start.10 = (s32[64]{0:T(128)S(1)}, s32[64]{0:T(128)}, u32[]{:S(2)}) copy-start(s32[64]{0:T(128)} %param.20) | copy-start | bytes 772
  223.4 9.2 %copy-start.8 = (f32[32]{0:T(128)S(1)}, f32[32]{0:T(128)}, u32[]{:S(2)}) copy-start(f32[32]{0:T(128)} %param.21) | copy-start | bytes 388
  231.2 8.9 %collective-permute-start = (bf16[896,2880]{0,1:T(8,128)(2,1)}, bf16[896,2880]{0,1:T(8,128)(2,1)}, u32[]{:S(2)}, u32[]{:S(2)}) collective-permute-start(bf16[896,2880]{0,1:T(8,128)(2,1)} %copy.34), channel_id=1, source_target_pairs={{0,1},{1,0},{2,3},{3,2},{4,5},{5,4},{6,7},{7,6},{8,9},{9,8},{10,11... | collective-permute-start | bytes 15482888 | tf_op jit(solution)/shard_map/ppermute | solution.py:159
  232.8 13.4 %copy-start.9 = (bf16[2880,4,128]{2,1,0:T(4,128)(2,1)S(1)}, bf16[2880,4,128]{2,1,0:T(4,128)(2,1)}, u32[]{:S(2)}) copy-start(bf16[2880,4,128]{2,1,0:T(4,128)(2,1)} %param.24) | copy-start | bytes 8847364
  246.1 3.4 copy-start.1
  346.6 16.5 %copy-start.6 = (bf16[2880]{0:T(1024)(128)(2,1)S(1)}, bf16[2880]{0:T(1024)(128)(2,1)}, u32[]{:S(2)}) copy-start(bf16[2880]{0:T(1024)(128)(2,1)} %param.26) | copy-start | bytes 17284
  363.0 8.9 %collective-permute-start.1 = (bf16[896,2880]{0,1:T(8,128)(2,1)}, bf16[896,2880]{0,1:T(8,128)(2,1)}, u32[]{:S(2)}, u32[]{:S(2)}) collective-permute-start(bf16[896,2880]{0,1:T(8,128)(2,1)} %convolution_convert_fusion.1), channel_id=1, source_target_pairs={{0,1},{1,0},{2,3},{3,2},{4,5},{5,4},{6,7},{7,6},{8,9},{9,8},{10,11... | collective-permute-start | bytes 15482888 | tf_op jit(solution)/shard_map/ppermute | solution.py:159
  382.3 13.6 %copy-start.2 = (bf16[896,2880]{0,1:T(8,128)(2,1)S(1)}, bf16[896,2880]{0,1:T(8,128)(2,1)}, u32[]{:S(2)}) copy-start(bf16[896,2880]{0,1:T(8,128)(2,1)} %get-tuple-element.12) | copy-start | bytes 15482884
  382.3 25.8 %slice-start = ((s8[8478720]{0:T(1024)(128)(4,1)}), s8[4194304]{0:T(1024)(128)(4,1)S(1)}, s32[]{:S(2)}) async-start(s8[8478720]{0:T(1024)(128)(4,1)} %bitcast.54), calls=%async_computation.3 | async-start | bytes 8388608
  382.3 25.8 %slice-start.1 = ((s8[8478720]{0:T(1024)(128)(4,1)}), s8[4194304]{0:T(1024)(128)(4,1)S(1)}, s32[]{:S(2)}) async-start(s8[8478720]{0:T(1024)(128)(4,1)} %bitcast.54), calls=%async_computation.4 | async-start | bytes 8388608
  395.8 12.2 %slice-start.2 = ((s8[8478720]{0:T(1024)(128)(4,1)}), s8[90112]{0:T(1024)(128)(4,1)S(1)}, s32[]{:S(2)}) async-start(s8[8478720]{0:T(1024)(128)(4,1)} %bitcast.54), calls=%async_computation.5 | async-start | bytes 180224
  418.0 2.3 copy-start
  422.0 5.1 collective-permute-start.2
  449.0 141.3 %all-to-all-start.1 = ((bf16[16,112,1440]{2,1,0:T(8,128)(2,1)}), bf16[16,112,1440]{2,1,0:T(8,128)(2,1)}, u32[]{:S(2)}, u32[]{:S(2)}) async-start(bf16[16,112,1440]{2,1,0:T(8,128)(2,1)} %broadcast_select_fusion), calls=%async_computation.1 | async-start | bytes 11010048 | tf_op jit(solution)/shard_map/all_to_all | solution.py:277
Sparse Core Ops, SparseCore 0:
  29.4 192.9 all-gather.1
